TPU v7x, 256 devices: a whole 4x4x8 slice. The times are simulated.
256 devices in a mesh: leaf: 64 (over x, z, core), rhs: 4 (over y).
Axes of the slice: x: 4, y: 4, z: 8, core: 2. Of those that a mesh axis runs over, the one named last changes fastest.
Arguments:
- values: float32 [16, 524288], P('rhs', 'leaf'), may hold values from -6 to 6
- geometry: float32 [7, 524288], P(None, ('leaf', 'rhs')), may hold values from -5 to 414, as said below
- basis: float32 [4096, 32, 128], P(('leaf', 'rhs')), may hold values from -0.5 to 0.5
- near: int32 [4096, 6], P('leaf'), may hold values from -1 to 4095, as said below
- transfer_one: float32 [2048, 2048], P('leaf'), may hold values from -0.75 to 0.75
- transfer_two: float32 [1024, 2048], P('leaf'), may hold values from -0.75 to 0.75
- couple_one: float32 [2048, 8192], P('leaf'), may hold values from -0.375 to 0.375
- couple_two: float32 [1024, 8192], P('leaf'), may hold values from -0.375 to 0.375
- lists_one: int32 [2048, 8], P('leaf'), may hold values from -1 to 2047, as said below
- lists_two: int32 [1024, 8], P('leaf'), may hold values from -1 to 1023, as said below
Outputs:
- applied: float32 [16, 524288], P('rhs', 'leaf')
Inputs may be any that keep to these rules, and one draw needn't show every extreme that they name: `geometry`: rows 0 to 2 are positions, rows 3 to 5 normal vectors not of unit length, row 6 positive weights. `near`: entry [i, j] is -1 (no partner) or a leaf within 16 leaves of i, and that distance is reached; entry [i, 0] is i; entries may repeat. `lists_one`: entry [t, j] is -1 (no partner) or a cluster of level one within 4 clusters of t, and that distance is reached; entries may repeat. `lists_two`: entry [t, j] is -1 (no partner) or any cluster of level two; entry [t, 0] is never -1; entries may repeat.
All inputs are finite; a program needn't handle non-finite values.
Results may differ from a plain program's by a relative error of at most 0.0003.
Values sent between devices are 32-bit elements; how exact they have to be, the bound alone decides.
No kernel may reach another device: no remote copies, remote signals or barrier semaphores. Data moves between devices by JAX's collectives and lax.ppermute only.
A program may use at most 192 MiB of HBM per device.

v0:
```python
import jax
import jax.numpy as jnp
from jax import lax
from jax.experimental import pallas as pl
from jax.experimental.pallas import tpu as pltpu
from jax.sharding import Mesh
from jax.sharding import PartitionSpec as P

PTS = 128
RANK = 32
NEAR = 6
COUPLE = 8
SOFTEN = 0.05
CONTRAST = 0.6
ROWS = 16
OWN = 16
F32 = jnp.float32
BF16 = jnp.bfloat16
ALL = ("x", "z", "c", "r")
VMEM = pl.BlockSpec(memory_space=pltpu.VMEM)
SMEM = pl.BlockSpec(memory_space=pltpu.SMEM)
PARAMS = pltpu.CompilerParams(vmem_limit_bytes=40 * 1024 * 1024)


def split(x):
    high = x.astype(BF16)
    return high, (x - high.astype(F32)).astype(BF16)


def dot(a, b):
    return jnp.dot(a, b, preferred_element_type=F32)


def dot_two(x, ones):
    high, low = split(x)
    return dot(high, ones) + dot(low, ones)


def lane_segment(rows):
    return lax.broadcasted_iota(jnp.int32, (rows, PTS), 1) // RANK


def fold(x):
    x = x + pltpu.roll(x, 64, 1)
    return x + pltpu.roll(x, 32, 1)


def summing():
    rows = lax.broadcasted_iota(jnp.int32, (1024, PTS), 0) // RANK
    lanes = lax.broadcasted_iota(jnp.int32, (1024, PTS), 1) % RANK
    return (rows == lanes).astype(F32).astype(BF16)


def spreading(segments):
    rows = lax.broadcasted_iota(jnp.int32, (PTS, 1024), 0)
    lanes = lax.broadcasted_iota(jnp.int32, (PTS, 1024), 1) // RANK
    return ((rows % RANK == lanes) & (rows < segments * RANK)).astype(F32).astype(BF16)


def pick(packed, segment, slot):
    return fold(jnp.where(segment == slot, packed, 0.0))


def own_half(ref, rank):
    return pltpu.roll(ref[0], (rank % 2) * 4, 0)


def up_kernel(place, v_ref, basis_ref, one_ref, two_ref, first_ref, last_ref, top_ref, leaf_c, one_c, sums, two_rows):
    rank = place[0]
    two_rows[...] = own_half(two_ref, rank)
    segment = lane_segment(ROWS)
    ones = summing()
    zeros = jnp.zeros((2 * RANK, PTS), BF16)
    for leaf in range(OWN):
        vh, vl = split(v_ref[:, leaf * PTS : (leaf + 1) * PTS])
        bh, bl = split(basis_ref[leaf])
        prod = lax.dot_general(
            jnp.concatenate([vh, vl], 0),
            jnp.concatenate([bh, bl, zeros], 0),
            (((1,), (1,)), ((), ())),
            preferred_element_type=F32,
        )
        leaf_c[leaf] = fold(prod[:ROWS] + prod[ROWS:])
    for t in range(8):
        for g in range(8):
            low, high = slice(g * PTS, (g + 1) * PTS), slice(1024 + g * PTS, 1024 + (g + 1) * PTS)
            sums[t * ROWS : (t + 1) * ROWS, low] = (
                one_ref[t : t + 1, low] * leaf_c[2 * t] + one_ref[t : t + 1, high] * leaf_c[2 * t + 1]
            )
    one_c[...] = dot_two(sums[...], ones)
    first = jnp.zeros((ROWS, PTS), F32)
    last = jnp.zeros((ROWS, PTS), F32)
    for t in range(4):
        first = jnp.where(segment == t, one_c[t * ROWS : (t + 1) * ROWS], first)
        last = jnp.where(segment == t, one_c[(t + 4) * ROWS : (t + 5) * ROWS], last)
    first_ref[...] = first
    last_ref[...] = last
    for t in range(4):
        for g in range(8):
            low, high = slice(g * PTS, (g + 1) * PTS), slice(1024 + g * PTS, 1024 + (g + 1) * PTS)
            sums[t * ROWS : (t + 1) * ROWS, low] = (
                two_rows[t : t + 1, low] * one_c[2 * t * ROWS : (2 * t + 1) * ROWS]
                + two_rows[t : t + 1, high] * one_c[(2 * t + 1) * ROWS : (2 * t + 2) * ROWS]
            )
    two = dot_two(sums[: 4 * ROWS], ones)
    top = jnp.zeros((ROWS, PTS), F32)
    for t in range(4):
        top = jnp.where(segment == t, two[t * ROWS : (t + 1) * ROWS], top)
    for copy in range(top_ref.shape[0]):
        top_ref[copy] = top


def couple_kernel(place, lists, mine_ref, other_ref, mats_ref, out0, out1, out2, out3, table, sums):
    rank, core = place[0], place[1]
    segment = lane_segment(ROWS)
    half = mine_ref.shape[0]
    table[:half] = mine_ref[...]
    table[half:] = other_ref[...]

    def body(block, _):
        for t in range(8):
            target = block * 8 + t
            step = target ^ (rank * 4)
            acc = [None] * 8
            for j in range(COUPLE):
                n = lists[target, j]
                live = (n >= 0) & (((n >> 2) & 3) == rank)
                group = jnp.where(live, n >> 4, 0)
                slot = jnp.where(live, n & 3, -1)
                coef = pick(table[((group & 1) ^ core) * half + (group >> 1)], segment, slot)
                for g in range(8):
                    row = mats_ref[block, t : t + 1, j * 1024 + g * PTS : j * 1024 + (g + 1) * PTS]
                    acc[g] = row * coef if j == 0 else acc[g] + row * coef
            for g in range(8):
                sums[pl.ds(pl.multiple_of(step * ROWS, ROWS), ROWS), g * PTS : (g + 1) * PTS] = acc[g]
        return 0

    lax.fori_loop(0, 2, body, 0)
    total = dot_two(sums[...], summing())
    for part, out in enumerate((out0, out1, out2, out3)):
        packed = jnp.zeros((ROWS, PTS), F32)
        for t in range(4):
            at = (part * 4 + t) * ROWS
            packed = jnp.where(segment == t, total[at : at + ROWS], packed)
        out[...] = packed


def near_kernel(place, near, g_left, g_own, g_right, v_left, v_own, v_right, out_ref, geo, weights):
    rank, base = place[0], place[2] * OWN - OWN
    zeros = jnp.zeros((PTS, ROWS), BF16)
    for s in range(3 * OWN):
        which, at = divmod(s, OWN)
        g_ref, v_ref = ((g_left, v_left), (g_own, v_own), (g_right, v_right))[which]
        cut = slice(at * PTS, (at + 1) * PTS)
        geo[s, 0:3] = g_ref[0:3, cut]
        geo[s, 3:6] = g_ref[3:6, cut] * CONTRAST
        scaled = v_ref[:, cut] * g_ref[6:7, cut]
        high = scaled.astype(BF16).astype(F32)
        turned = jnp.transpose(jnp.concatenate([high, scaled - high], 0)).astype(BF16)
        weights[s, 0:PTS] = turned
        weights[s, PTS : 2 * PTS] = jnp.concatenate([turned[:, :ROWS], zeros], 1)
    geo[3 * OWN] = jnp.zeros((8, PTS), F32)
    weights[3 * OWN] = jnp.zeros((2 * PTS, 2 * ROWS), BF16)

    def body(i, _):
        own = jnp.transpose(geo[OWN + i])
        px = jnp.broadcast_to(own[:, 0:1], (PTS, PTS))
        py = jnp.broadcast_to(own[:, 1:2], (PTS, PTS))
        pz = jnp.broadcast_to(own[:, 2:3], (PTS, PTS))
        total = jnp.zeros((PTS, 2 * ROWS), F32)
        for j in range(NEAR):
            n = near[rank * OWN + i, j]
            s = jnp.where(n >= 0, jnp.clip(n - base, 0, 3 * OWN - 1), 3 * OWN)
            src = geo[s]
            dx, dy, dz = px - src[0:1], py - src[1:2], pz - src[2:3]
            inv = lax.rsqrt(dx * dx + dy * dy + dz * dz + SOFTEN)
            turn = dx * src[3:4] + dy * src[4:5] + dz * src[5:6]
            value = inv + turn * (inv * inv * inv)
            high, low = split(value)
            total = total + dot(jnp.concatenate([high, low], 1), weights[s])
        flat = jnp.transpose(total)
        out_ref[:, pl.ds(pl.multiple_of(i * PTS, PTS), PTS)] = flat[:ROWS] + flat[ROWS:]
        return 0

    lax.fori_loop(0, OWN, body, 0)


def final_kernel(
    place, lists, part0, part1, part2, part3, left, first, last, right,
    one_ref, two_ref, mats_ref, basis_ref, near_ref, out_ref, table, sums, spread, two_rows,
):
    rank, base = place[0], place[2] * 8 - 4
    two_rows[...] = own_half(two_ref, rank)
    segment = lane_segment(ROWS)
    for at, ref in enumerate((left, first, last, right)):
        table[at] = ref[...]

    for t in range(8):
        acc = [None] * 8
        for j in range(COUPLE):
            n = lists[rank * 8 + t, j]
            q = jnp.clip(n - base, 0, 15)
            slot = jnp.where(n >= 0, q & 3, -1)
            coef = pick(table[q >> 2], segment, slot)
            for g in range(8):
                row = mats_ref[t : t + 1, j * 1024 + g * PTS : j * 1024 + (g + 1) * PTS]
                acc[g] = row * coef if j == 0 else acc[g] + row * coef
        for g in range(8):
            sums[t * ROWS : (t + 1) * ROWS, g * PTS : (g + 1) * PTS] = acc[g]
    mid = dot_two(sums[...], summing())
    down = part0[...] + part1[...] + part2[...] + part3[...]
    rows = jnp.concatenate([jnp.where(segment == t, down, 0.0) for t in range(4)], 0)
    spread[: 4 * ROWS] = dot_two(rows, spreading(4))
    mids = []
    for t in range(4):
        for k in range(2):
            acc = None
            for g in range(8):
                lanes = slice(g * PTS, (g + 1) * PTS)
                row = two_rows[t : t + 1, k * 1024 + g * PTS : k * 1024 + (g + 1) * PTS]
                term = row * spread[t * ROWS : (t + 1) * ROWS, lanes]
                acc = term if g == 0 else acc + term
            at = (2 * t + k) * ROWS
            mids.append(mid[at : at + ROWS] + fold(acc))
    spread[...] = dot_two(jnp.concatenate(mids, 0), spreading(1))
    zeros = jnp.zeros((RANK, PTS), BF16)
    for t in range(8):
        for k in range(2):
            acc = None
            for g in range(8):
                lanes = slice(g * PTS, (g + 1) * PTS)
                row = one_ref[t : t + 1, k * 1024 + g * PTS : k * 1024 + (g + 1) * PTS]
                term = row * spread[t * ROWS : (t + 1) * ROWS, lanes]
                acc = term if g == 0 else acc + term
            down_leaf = fold(acc)
            leaf = 2 * t + k
            high = down_leaf.astype(BF16).astype(F32)
            low = down_leaf - high
            lhs = jnp.where(segment == 1, low, jnp.where(segment == 3, 0.0, high)).astype(BF16)
            bh, bl = split(basis_ref[leaf])
            far = dot(lhs, jnp.concatenate([bh, bh, bl, zeros], 0))
            cut = slice(leaf * PTS, (leaf + 1) * PTS)
            out_ref[:, cut] = near_ref[:, cut] + far


def shape(*dims):
    return jax.ShapeDtypeStruct(dims, F32)


def on_device(values, geometry, basis, near, transfer_one, transfer_two, couple_one, couple_two, lists_one, lists_two):
    size = lax.axis_size("x") * lax.axis_size("z") * lax.axis_size("c") * lax.axis_size("r")
    gathered = lax.axis_size("x") * lax.axis_size("z")
    place = jnp.stack([lax.axis_index("r"), lax.axis_index("c"), lax.axis_index(ALL)]).astype(jnp.int32)
    up_by_one = [(i, i + 1) for i in range(size - 1)]
    down_by_one = [(i + 1, i) for i in range(size - 1)]

    def both(low, high):
        return lax.ppermute(high, ALL, up_by_one), lax.ppermute(low, ALL, down_by_one)

    geo_left, geo_right = both(geometry, geometry)
    val = lax.all_to_all(values, "r", split_axis=1, concat_axis=0, tiled=True)
    val_left, val_right = both(val, val)

    def rows_of(height, width):
        return pl.BlockSpec((height, width), lambda i, place: (place[0], 0))

    def whole(*dims):
        return pl.BlockSpec(dims, lambda i, place: (0,) * len(dims))

    two_of = pl.BlockSpec((1, 8, 2048), lambda i, place: (place[0] // 2, 0, 0))
    transfer_two = transfer_two.reshape(2, 8, 2048)
    couple_two = couple_two.reshape(2, 8, 8192)

    first, last, top = pl.pallas_call(
        up_kernel,
        grid_spec=pltpu.PrefetchScalarGridSpec(
            num_scalar_prefetch=1,
            grid=(1,),
            in_specs=[whole(ROWS, OWN * PTS), whole(OWN, RANK, PTS), rows_of(8, 2048), two_of],
            out_specs=[whole(ROWS, PTS), whole(ROWS, PTS), whole(gathered, ROWS, PTS)],
            scratch_shapes=[
                pltpu.VMEM((OWN, ROWS, PTS), F32),
                pltpu.VMEM((8 * ROWS, PTS), F32),
                pltpu.VMEM((8 * ROWS, 1024), F32),
                pltpu.VMEM((8, 2048), F32),
            ],
        ),
        out_shape=[shape(ROWS, PTS), shape(ROWS, PTS), shape(gathered, ROWS, PTS)],
        compiler_params=PARAMS,
        cost_estimate=pl.CostEstimate(flops=40_000_000, bytes_accessed=600_000, transcendentals=0),
    )(place, val, basis, transfer_one, transfer_two)

    mine = lax.all_to_all(top, ("x", "z"), split_axis=0, concat_axis=0, tiled=True)
    other = lax.ppermute(mine, "c", [(0, 1), (1, 0)])
    left, right = both(first, last)

    parts = pl.pallas_call(
        couple_kernel,
        in_specs=[SMEM, SMEM, VMEM, VMEM, VMEM],
        out_specs=[VMEM] * 4,
        out_shape=[shape(ROWS, PTS)] * 4,
        scratch_shapes=[pltpu.VMEM((2 * gathered, ROWS, PTS), F32), pltpu.VMEM((16 * ROWS, 1024), F32)],
        compiler_params=PARAMS,
        cost_estimate=pl.CostEstimate(flops=100_000_000, bytes_accessed=1_000_000, transcendentals=0),
    )(place, lists_two, mine, other, couple_two)
    received = [parts[0]]
    for s in range(1, 4):
        received.append(lax.ppermute(parts[s], "r", [(i, i ^ s) for i in range(4)]))

    near_part = pl.pallas_call(
        near_kernel,
        in_specs=[SMEM, SMEM] + [VMEM] * 6,
        out_specs=VMEM,
        out_shape=shape(ROWS, OWN * PTS),
        scratch_shapes=[
            pltpu.VMEM((3 * OWN + 1, 8, PTS), F32),
            pltpu.VMEM((3 * OWN + 1, 2 * PTS, 2 * ROWS), BF16),
        ],
        compiler_params=PARAMS,
        cost_estimate=pl.CostEstimate(flops=3_000_000_000, bytes_accessed=700_000, transcendentals=1_600_000),
    )(place, near, geo_left, geometry, geo_right, val_left, val, val_right)

    result = pl.pallas_call(
        final_kernel,
        grid_spec=pltpu.PrefetchScalarGridSpec(
            num_scalar_prefetch=1,
            grid=(1,),
            in_specs=[SMEM]
            + [whole(ROWS, PTS)] * 8
            + [rows_of(8, 2048), two_of, rows_of(8, 8192), whole(OWN, RANK, PTS), whole(ROWS, OWN * PTS)],
            out_specs=whole(ROWS, OWN * PTS),
            scratch_shapes=[
                pltpu.VMEM((4, ROWS, PTS), F32),
                pltpu.VMEM((8 * ROWS, 1024), F32),
                pltpu.VMEM((8 * ROWS, 1024), F32),
                pltpu.VMEM((8, 2048), F32),
            ],
        ),
        out_shape=shape(ROWS, OWN * PTS),
        compiler_params=PARAMS,
        cost_estimate=pl.CostEstimate(flops=40_000_000, bytes_accessed=1_000_000, transcendentals=0),
    )(
        place, lists_one, *received, left, first, last, right,
        transfer_one, transfer_two, couple_one, basis, near_part,
    )
    return lax.all_to_all(result, "r", split_axis=0, concat_axis=1, tiled=True)


def solution(mesh):
    fine = Mesh(mesh.devices.reshape(4, 8, 2, 4), ALL)
    leaf = ("x", "z", "c")
    return jax.shard_map(
        on_device,
        mesh=fine,
        in_specs=(
            P("r", leaf),
            P(None, ALL),
            P(ALL, None, None),
            P(leaf, None),
            P(leaf, None),
            P(leaf, None),
            P(leaf, None),
            P(leaf, None),
            P(leaf, None),
            P(leaf, None),
        ),
        out_specs=P("r", leaf),
        check_vma=False,
    )
```

profile of v0, /device:TPU:2, one launch (start us, length us, event | category | flops | bytes accessed | tf_op | source)
XLA Modules:
  0.0 99.1 jit_solution(5952085325349443487)
XLA Ops:
  0.0 0.0 copy-start.1
  0.0 0.0 copy-start.2
  0.0 4.6 %all-to-all-start = ((f32[4,4,2048]{2,0,1:T(4,128)}), f32[4,4,2048]{2,0,1:T(4,128)S(1)}, u32[]{:S(2)}, u32[]{:S(2)}) async-start(f32[4,4,2048]{2,0,1:T(4,128)} %bitcast.15), calls=%async_computation | async-start | bytes 262144 | tf_op jit(solution)/shard_map/all_to_all | solution.py:261
  4.6 0.1 pad_add_fusion.place
  4.7 5.9 %all-to-all-done = f32[4,4,2048]{2,0,1:T(4,128)S(1)} async-done(((f32[4,4,2048]{2,0,1:T(4,128)}), f32[4,4,2048]{2,0,1:T(4,128)S(1)}, u32[]{:S(2)}, u32[]{:S(2)}) %all-to-all-start) | async-done | bytes 131104 | tf_op jit(solution)/shard_map/all_to_all | solution.py:261
  10.6 0.0 copy-done.1
  10.6 0.0 copy-done.2
  10.6 0.0 copy-start.3
  10.7 0.9 copy-done.3
  11.6 0.0 copy-start.5
  11.6 1.4 %shard_map.100 = (f32[16,128]{1,0:T(8,128)S(1)}, f32[16,128]{1,0:T(8,128)S(1)}, f32[32,16,128]{2,1,0:T(8,128)S(1)}) custom-call(s32[3]{0:T(128)S(1)} %pad_add_fusion.place, f32[16,2048]{1,0:T(8,128)S(1)} %all_to_all.34.v_ref.v_own, f32[16,32,128]{2,1,0:T(8,128)S(1)} %copy-done.1, f32[32,2048]{1,0:T(8,128)S(1)} %copy-done.2, f32[2,8,2048]{2,1,0:T(8,128)S(1)} %bitcast.10), custom_call_target="tpu_custom_call" | custom-call | flops 40000000 | bytes 600000 | tf_op jit(solution)/shard_map/pallas_call | solution.py:274
  13.0 0.0 copy-start.6
  13.0 0.0 copy-start.7
  13.0 21.7 %all_to_all.43.mine_ref = f32[32,16,128]{2,1,0:T(8,128)S(1)} all-to-all(f32[32,16,128]{2,1,0:T(8,128)S(1)} %get-tuple-element.12), channel_id=1, replica_groups=mesh['x'=4,'z'=8,'c'=2,'r'=4] {'x','z'}, dimensions={0} | all-to-all | bytes 524288 | tf_op jit(solution)/shard_map/all_to_all | solution.py:293
  34.7 0.0 copy-start.8
  34.7 0.0 collective-permute-start
  34.7 2.6 %collective-permute-start.8 = (f32[16,2048]{1,0:T(8,128)S(1)}, f32[16,2048]{1,0:T(8,128)S(1)}, u32[]{:S(2)}, u32[]{:S(2)}) collective-permute-start(f32[16,2048]{1,0:T(8,128)S(1)} %all_to_all.34.v_ref.v_own), channel_id=1, source_target_pairs={{0,1},{1,2},{2,3},{3,4},{4,5},{5,6},{6,7},{7,8},{8,9},{9,10},{10,1... | collective-permute-start | bytes 393224 | tf_op jit(solution)/shard_map/ppermute | solution.py:258
  37.4 7.3 %collective-permute-start.9 = (f32[16,2048]{1,0:T(8,128)S(1)}, f32[16,2048]{1,0:T(8,128)S(1)}, u32[]{:S(2)}, u32[]{:S(2)}) collective-permute-start(f32[16,2048]{1,0:T(8,128)S(1)} %all_to_all.34.v_ref.v_own), channel_id=1, source_target_pairs={{1,0},{2,1},{3,2},{4,3},{5,4},{6,5},{7,6},{8,7},{9,8},{10,9},{11,1... | collective-permute-start | bytes 393224 | tf_op jit(solution)/shard_map/ppermute | solution.py:258
  44.7 0.0 copy-done.6
  44.7 1.9 %collective-permute-start.6 = (f32[7,2048]{1,0:T(8,128)S(1)}, f32[7,2048]{1,0:T(8,128)S(1)}, u32[]{:S(2)}, u32[]{:S(2)}) collective-permute-start(f32[7,2048]{1,0:T(8,128)S(1)} %copy-done.6), channel_id=1, source_target_pairs={{0,1},{1,2},{2,3},{3,4},{4,5},{5,6},{6,7},{7,8},{8,9},{9,10},{10,1... | collective-permute-start | bytes 172040 | tf_op jit(solution)/shard_map/ppermute | solution.py:258
  46.6 7.9 %collective-permute-start.7 = (f32[7,2048]{1,0:T(8,128)S(1)}, f32[7,2048]{1,0:T(8,128)S(1)}, u32[]{:S(2)}, u32[]{:S(2)}) collective-permute-start(f32[7,2048]{1,0:T(8,128)S(1)} %copy-done.6), channel_id=1, source_target_pairs={{1,0},{2,1},{3,2},{4,3},{5,4},{6,5},{7,6},{8,7},{9,8},{10,9},{11,1... | collective-permute-start | bytes 172040 | tf_op jit(solution)/shard_map/ppermute | solution.py:258
  54.5 0.0 copy-done.7
  54.5 0.1 copy.12.lists
  54.5 0.0 copy-done.8
  54.5 0.0 copy-start.9
  54.5 0.1 copy.13.near
  54.6 0.6 copy-done.9
  55.2 0.1 copy.14.lists
  55.3 0.0 collective-permute-done.other_ref
  55.3 1.9 %collective-permute-start.4 = (f32[16,128]{1,0:T(8,128)S(1)}, f32[16,128]{1,0:T(8,128)S(1)}, u32[]{:S(2)}, u32[]{:S(2)}) collective-permute-start(f32[16,128]{1,0:T(8,128)S(1)} %get-tuple-element.17.last), channel_id=1, source_target_pairs={{0,1},{1,2},{2,3},{3,4},{4,5},{5,6},{6,7},{7,8},{8,9},{9,10},{10,1... | collective-permute-start | bytes 24584 | tf_op jit(solution)/shard_map/ppermute | solution.py:258
  57.2 0.0 copy-done.5
  57.2 5.5 %shard_map.101 = (f32[16,128]{1,0:T(8,128)S(1)}, f32[16,128]{1,0:T(8,128)S(1)}, f32[16,128]{1,0:T(8,128)S(1)}, f32[16,128]{1,0:T(8,128)S(1)}) custom-call(s32[3]{0:T(128)S(1)} %pad_add_fusion.place, s32[16,8]{1,0:T(8,128)S(1)} %copy.12.lists, f32[32,16,128]{2,1,0:T(8,128)S(1)} %all_to_all.43.mine_ref, f32[32,16,128]{2,1,0:T(8,128)S(1)} %collective-permute-done.other_ref, ...), custom_call_target="tpu_custom_call" | custom-call | flops 100000000 | bytes 1000000 | tf_op jit(solution)/shard_map/pallas_call | solution.py:297
  62.8 0.0 collective-permute-done.6.g_left
  62.8 7.9 %collective-permute-start.5 = (f32[16,128]{1,0:T(8,128)S(1)}, f32[16,128]{1,0:T(8,128)S(1)}, u32[]{:S(2)}, u32[]{:S(2)}) collective-permute-start(f32[16,128]{1,0:T(8,128)S(1)} %get-tuple-element.18.first), channel_id=1, source_target_pairs={{1,0},{2,1},{3,2},{4,3},{5,4},{6,5},{7,6},{8,7},{9,8},{10,9},{11,1... | collective-permute-start | bytes 24584 | tf_op jit(solution)/shard_map/ppermute | solution.py:258
  70.7 0.0 collective-permute-done.7.g_right
  70.7 0.1 collective-permute-start.1
  70.8 0.0 collective-permute-done.8.v_left
  70.8 0.1 collective-permute-start.2
  70.9 0.0 collective-permute-done.9.v_right
  70.9 0.0 copy-start
  70.9 0.0 copy-start.4
  70.9 4.6 %collective-permute-start.3 = (f32[16,128]{1,0:T(8,128)S(1)}, f32[16,128]{1,0:T(8,128)S(1)}, u32[]{:S(2)}, u32[]{:S(2)}) collective-permute-start(f32[16,128]{1,0:T(8,128)S(1)} %get-tuple-element.16), channel_id=1, source_target_pairs={{0,3},{1,2},{2,1},{3,0},{4,7},{5,6},{6,5},{7,4},{8,11},{9,10},{10,... | collective-permute-start | bytes 24584 | tf_op jit(solution)/shard_map/ppermute | solution.py:308
  75.5 11.4 %shard_map.102.near_ref = f32[16,2048]{1,0:T(8,128)S(1)} custom-call(s32[3]{0:T(128)S(1)} %pad_add_fusion.place, s32[64,6]{1,0:T(8,128)S(1)} %copy.13.near, f32[7,2048]{1,0:T(8,128)S(1)} %collective-permute-done.6.g_left, f32[7,2048]{1,0:T(8,128)S(1)} %copy-done.6, f32[7,2048]{1,0:T(8,128)S(1)} %collective-permute-done.7.g_right, ...), custom_call_target="tpu_custom_call" | custom-call | flops 3000000000 | bytes 700000 | tf_op jit(solution)/shard_map/pallas_call | solution.py:310
  86.9 0.0 collective-permute-done.4.left
  86.9 0.0 collective-permute-done.5.right
  86.9 0.0 collective-permute-done.1.part1
  86.9 0.0 collective-permute-done.2.part2
  86.9 0.0 collective-permute-done.3.part3
  86.9 0.0 copy-done
  86.9 0.0 copy-done.4
  87.0 3.1 %shard_map.103 = f32[16,2048]{1,0:T(8,128)S(1)} custom-call(s32[3]{0:T(128)S(1)} %pad_add_fusion.place, s32[32,8]{1,0:T(8,128)S(1)} %copy.14.lists, f32[16,128]{1,0:T(8,128)S(1)} %get-tuple-element.13.part0, f32[16,128]{1,0:T(8,128)S(1)} %collective-permute-done.1.part1, f32[16,128]{1,0:T(8,128)S(1)} %collective-permute-done.2.part2, ...), custom_call_target="tpu_custom_call" | custom-call | flops 40000000 | bytes 1000000 | tf_op jit(solution)/shard_map/pallas_call | solution.py:323
  90.1 8.4 %all_to_all.44 = f32[4,4,2048]{2,1,0:T(4,128)S(1)} all-to-all(f32[4,4,2048]{2,1,0:T(4,128)S(1)} %all_to_all.36), channel_id=1, replica_groups=mesh['x'=4,'z'=8,'c'=2,'r'=4] {'r'}, dimensions={0} | all-to-all | bytes 262144 | tf_op jit(solution)/shard_map/all_to_all | solution.py:346
  98.5 0.7 copy.17
  (2 shorter events, 0.1 us)
Async XLA Ops:
  0.0 10.6 %copy-start.1 = (f32[16,32,128]{2,1,0:T(8,128)S(1)}, f32[16,32,128]{2,1,0:T(8,128)}, u32[]{:S(2)}) copy-start(f32[16,32,128]{2,1,0:T(8,128)} %basis_ref.3) | copy-start | bytes 786436
  0.0 10.6 %copy-start.2 = (f32[32,2048]{1,0:T(8,128)S(1)}, f32[32,2048]{1,0:T(8,128)}, u32[]{:S(2)}) copy-start(f32[32,2048]{1,0:T(8,128)} %one_ref.3) | copy-start | bytes 786436
  0.0 10.6 %all-to-all-start = ((f32[4,4,2048]{2,0,1:T(4,128)}), f32[4,4,2048]{2,0,1:T(4,128)S(1)}, u32[]{:S(2)}, u32[]{:S(2)}) async-start(f32[4,4,2048]{2,0,1:T(4,128)} %bitcast.15), calls=%async_computation | async-start | bytes 262144 | tf_op jit(solution)/shard_map/all_to_all | solution.py:261
  10.6 0.9 copy-start.3
  11.6 45.7 %copy-start.5 = (f32[16,8192]{1,0:T(8,128)S(1)}, f32[16,8192]{1,0:T(8,128)}, u32[]{:S(2)}) copy-start(f32[16,8192]{1,0:T(8,128)} %param.17) | copy-start | bytes 1572868
  13.0 31.7 %copy-start.6 = (f32[7,2048]{1,0:T(8,128)S(1)}, f32[7,2048]{1,0:T(8,128)}, u32[]{:S(2)}) copy-start(f32[7,2048]{1,0:T(8,128)} %g_own.1) | copy-start | bytes 172036
  13.0 41.5 %copy-start.7 = (s32[16,8]{0,1:T(8,128)S(1)}, s32[16,8]{0,1:T(8,128)}, u32[]{:S(2)}) copy-start(s32[16,8]{0,1:T(8,128)} %param.19) | copy-start | bytes 1540
  34.7 19.8 %copy-start.8 = (s32[64,6]{0,1:T(8,128)S(1)}, s32[64,6]{0,1:T(8,128)}, u32[]{:S(2)}) copy-start(s32[64,6]{0,1:T(8,128)} %param.13) | copy-start | bytes 4612
  34.7 20.6 %collective-permute-start = (f32[32,16,128]{2,1,0:T(8,128)S(1)}, f32[32,16,128]{2,1,0:T(8,128)S(1)}, u32[]{:S(2)}, u32[]{:S(2)}) collective-permute-start(f32[32,16,128]{2,1,0:T(8,128)S(1)} %all_to_all.43.mine_ref), channel_id=1, source_target_pairs={{0,4},{4,0},{1,5},{5,1},{2,6},{6,2},{3,7},{7,3},{8,12},{12,8},{9,1... | collective-permute-start | bytes 786440 | tf_op jit(solution)/shard_map/ppermute | solution.py:294
  34.7 36.1 %collective-permute-start.8 = (f32[16,2048]{1,0:T(8,128)S(1)}, f32[16,2048]{1,0:T(8,128)S(1)}, u32[]{:S(2)}, u32[]{:S(2)}) collective-permute-start(f32[16,2048]{1,0:T(8,128)S(1)} %all_to_all.34.v_ref.v_own), channel_id=1, source_target_pairs={{0,1},{1,2},{2,3},{3,4},{4,5},{5,6},{6,7},{7,8},{8,9},{9,10},{10,1... | collective-permute-start | bytes 393224 | tf_op jit(solution)/shard_map/ppermute | solution.py:258
  37.4 33.5 %collective-permute-start.9 = (f32[16,2048]{1,0:T(8,128)S(1)}, f32[16,2048]{1,0:T(8,128)S(1)}, u32[]{:S(2)}, u32[]{:S(2)}) collective-permute-start(f32[16,2048]{1,0:T(8,128)S(1)} %all_to_all.34.v_ref.v_own), channel_id=1, source_target_pairs={{1,0},{2,1},{3,2},{4,3},{5,4},{6,5},{7,6},{8,7},{9,8},{10,9},{11,1... | collective-permute-start | bytes 393224 | tf_op jit(solution)/shard_map/ppermute | solution.py:258
  44.7 18.1 %collective-permute-start.6 = (f32[7,2048]{1,0:T(8,128)S(1)}, f32[7,2048]{1,0:T(8,128)S(1)}, u32[]{:S(2)}, u32[]{:S(2)}) collective-permute-start(f32[7,2048]{1,0:T(8,128)S(1)} %copy-done.6), channel_id=1, source_target_pairs={{0,1},{1,2},{2,3},{3,4},{4,5},{5,6},{6,7},{7,8},{8,9},{9,10},{10,1... | collective-permute-start | bytes 172040 | tf_op jit(solution)/shard_map/ppermute | solution.py:258
  46.6 24.1 %collective-permute-start.7 = (f32[7,2048]{1,0:T(8,128)S(1)}, f32[7,2048]{1,0:T(8,128)S(1)}, u32[]{:S(2)}, u32[]{:S(2)}) collective-permute-start(f32[7,2048]{1,0:T(8,128)S(1)} %copy-done.6), channel_id=1, source_target_pairs={{1,0},{2,1},{3,2},{4,3},{5,4},{6,5},{7,6},{8,7},{9,8},{10,9},{11,1... | collective-permute-start | bytes 172040 | tf_op jit(solution)/shard_map/ppermute | solution.py:258
  54.5 0.7 copy-start.9
  55.3 31.6 %collective-permute-start.4 = (f32[16,128]{1,0:T(8,128)S(1)}, f32[16,128]{1,0:T(8,128)S(1)}, u32[]{:S(2)}, u32[]{:S(2)}) collective-permute-start(f32[16,128]{1,0:T(8,128)S(1)} %get-tuple-element.17.last), channel_id=1, source_target_pairs={{0,1},{1,2},{2,3},{3,4},{4,5},{5,6},{6,7},{7,8},{8,9},{9,10},{10,1... | collective-permute-start | bytes 24584 | tf_op jit(solution)/shard_map/ppermute | solution.py:258
  62.8 24.1 %collective-permute-start.5 = (f32[16,128]{1,0:T(8,128)S(1)}, f32[16,128]{1,0:T(8,128)S(1)}, u32[]{:S(2)}, u32[]{:S(2)}) collective-permute-start(f32[16,128]{1,0:T(8,128)S(1)} %get-tuple-element.18.first), channel_id=1, source_target_pairs={{1,0},{2,1},{3,2},{4,3},{5,4},{6,5},{7,6},{8,7},{9,8},{10,9},{11,1... | collective-permute-start | bytes 24584 | tf_op jit(solution)/shard_map/ppermute | solution.py:258
  70.7 16.2 %collective-permute-start.1 = (f32[16,128]{1,0:T(8,128)S(1)}, f32[16,128]{1,0:T(8,128)S(1)}, u32[]{:S(2)}, u32[]{:S(2)}) collective-permute-start(f32[16,128]{1,0:T(8,128)S(1)} %get-tuple-element.14), channel_id=1, source_target_pairs={{0,1},{1,0},{2,3},{3,2},{4,5},{5,4},{6,7},{7,6},{8,9},{9,8},{10,11... | collective-permute-start | bytes 24584 | tf_op jit(solution)/shard_map/ppermute | solution.py:308
  70.8 16.1 %collective-permute-start.2 = (f32[16,128]{1,0:T(8,128)S(1)}, f32[16,128]{1,0:T(8,128)S(1)}, u32[]{:S(2)}, u32[]{:S(2)}) collective-permute-start(f32[16,128]{1,0:T(8,128)S(1)} %get-tuple-element.15), channel_id=1, source_target_pairs={{0,2},{1,3},{2,0},{3,1},{4,6},{5,7},{6,4},{7,5},{8,10},{9,11},{10,... | collective-permute-start | bytes 24584 | tf_op jit(solution)/shard_map/ppermute | solution.py:308
  70.9 16.0 %copy-start = (f32[32,8192]{1,0:T(8,128)S(1)}, f32[32,8192]{1,0:T(8,128)}, u32[]{:S(2)}) copy-start(f32[32,8192]{1,0:T(8,128)} %mats_ref.1) | copy-start | bytes 3145732
  70.9 16.0 %copy-start.4 = (f32[16,2048]{1,0:T(8,128)S(1)}, f32[16,2048]{1,0:T(8,128)}, u32[]{:S(2)}) copy-start(f32[16,2048]{1,0:T(8,128)} %param.15) | copy-start | bytes 393220
  70.9 16.0 %collective-permute-start.3 = (f32[16,128]{1,0:T(8,128)S(1)}, f32[16,128]{1,0:T(8,128)S(1)}, u32[]{:S(2)}, u32[]{:S(2)}) collective-permute-start(f32[16,128]{1,0:T(8,128)S(1)} %get-tuple-element.16), channel_id=1, source_target_pairs={{0,3},{1,2},{2,1},{3,0},{4,7},{5,6},{6,5},{7,4},{8,11},{9,10},{10,... | collective-permute-start | bytes 24584 | tf_op jit(solution)/shard_map/ppermute | solution.py:308
where the time goes:
time: 99.6 us; the launch traced here: 99.1 us
  starting transfers between devices  38.8 us (39%)
  blocking collectives  30.1 us (30%)
  Pallas kernels  21.5 us (22%)
  waiting for transfers between devices  5.93 us (6%)
  local copies, waits for them, and re-layouts  2.52 us (3%)
    ppermute x3, starting transfers between devices, both(): lax.ppermute(low, ALL, down_by_one)  23 us
    all_to_all x1, blocking collectives, on_device(): lax.all_to_all(top, ('x', 'z'), split_axis=0, concat_axis=0, tiled=True)  21.7 us
    pallas_call x1, Pallas kernels, on_device(): pl.pallas_call(near_kernel, in_specs=[SMEM, SMEM] + [VMEM] * 6, out_specs...  11.4 us
    all_to_all x1, blocking collectives, on_device(): return lax.all_to_all(result, 'r', split_axis=0, concat_axis=1, tiled=True)  8.36 us
    ppermute x3, starting transfers between devices, both(): lax.ppermute(high, ALL, up_by_one)  6.44 us
    all_to_all x1, waiting for transfers between devices, on_device(): val = lax.all_to_all(values, 'r', split_axis=1, concat_axis=0, tiled=True)  5.9 us
    pallas_call x1, Pallas kernels, on_device(): pl.pallas_call(couple_kernel, in_specs=[SMEM, SMEM, VMEM, VMEM, VMEM], ou...  5.55 us
    ppermute x3, starting transfers between devices, on_device(): received.append(lax.ppermute(parts[s], 'r', [(i, i ^ s) for i in range(4)]))  4.74 us
  transfers between devices with their start and end apart: 11, of which 1 were waited for; matrix products, arithmetic and copies ran while one was open for 0% of the time, Pallas kernels for 17%

commit v1 on v0

--- a/solution.py
+++ b/solution.py
@@ -14,6 +14,9 @@
 CONTRAST = 0.6
 ROWS = 16
 OWN = 16
+FIRST = slice(OWN * PTS, OWN * PTS + PTS)
+LAST = slice(OWN * PTS + PTS, OWN * PTS + 2 * PTS)
+STRIP = (ROWS + 8, OWN * PTS + 2 * PTS)
 F32 = jnp.float32
 BF16 = jnp.bfloat16
 ALL = ("x", "z", "c", "r")
@@ -65,9 +68,11 @@
     return pltpu.roll(ref[0], (rank % 2) * 4, 0)
 
 
-def up_kernel(place, v_ref, basis_ref, one_ref, two_ref, first_ref, last_ref, top_ref, leaf_c, one_c, sums, two_rows):
+def up_kernel(place, v_ref, geo_ref, basis_ref, one_ref, two_ref, strip_ref, top_ref, leaf_c, one_c, sums, two_rows):
     rank = place[0]
     two_rows[...] = own_half(two_ref, rank)
+    strip_ref[:ROWS, : OWN * PTS] = v_ref[...]
+    strip_ref[ROWS : ROWS + 7, : OWN * PTS] = geo_ref[...]
     segment = lane_segment(ROWS)
     ones = summing()
     zeros = jnp.zeros((2 * RANK, PTS), BF16)
@@ -93,8 +98,8 @@
     for t in range(4):
         first = jnp.where(segment == t, one_c[t * ROWS : (t + 1) * ROWS], first)
         last = jnp.where(segment == t, one_c[(t + 4) * ROWS : (t + 5) * ROWS], last)
-    first_ref[...] = first
-    last_ref[...] = last
+    strip_ref[:ROWS, FIRST] = first
+    strip_ref[:ROWS, LAST] = last
     for t in range(4):
         for g in range(8):
             low, high = slice(g * PTS, (g + 1) * PTS), slice(1024 + g * PTS, 1024 + (g + 1) * PTS)
@@ -110,51 +115,52 @@
         top_ref[copy] = top
 
 
-def couple_kernel(place, lists, mine_ref, other_ref, mats_ref, out0, out1, out2, out3, table, sums):
+def couple_kernel(place, lists, mine_ref, other_ref, mats_ref, out_ref, table, sums):
     rank, core = place[0], place[1]
     segment = lane_segment(ROWS)
     half = mine_ref.shape[0]
     table[:half] = mine_ref[...]
     table[half:] = other_ref[...]
+    sums[...] = jnp.zeros(sums.shape, F32)
 
     def body(block, _):
         for t in range(8):
             target = block * 8 + t
-            step = target ^ (rank * 4)
-            acc = [None] * 8
+            rows = pl.ds(pl.multiple_of(target * ROWS, ROWS), ROWS)
+            entries = [lists[target, j] for j in range(COUPLE)]
+            lives = [(n >= 0) & (((n >> 2) & 3) == rank) for n in entries]
             for j in range(COUPLE):
-                n = lists[target, j]
-                live = (n >= 0) & (((n >> 2) & 3) == rank)
-                group = jnp.where(live, n >> 4, 0)
-                slot = jnp.where(live, n & 3, -1)
-                coef = pick(table[((group & 1) ^ core) * half + (group >> 1)], segment, slot)
-                for g in range(8):
-                    row = mats_ref[block, t : t + 1, j * 1024 + g * PTS : j * 1024 + (g + 1) * PTS]
-                    acc[g] = row * coef if j == 0 else acc[g] + row * coef
-            for g in range(8):
-                sums[pl.ds(pl.multiple_of(step * ROWS, ROWS), ROWS), g * PTS : (g + 1) * PTS] = acc[g]
+
+                @pl.when(lives[j])
+                def _(j=j, n=entries[j]):
+                    group = n >> 4
+                    coef = pick(table[((group & 1) ^ core) * half + (group >> 1)], segment, n & 3)
+                    for g in range(8):
+                        row = mats_ref[block, t : t + 1, j * 1024 + g * PTS : j * 1024 + (g + 1) * PTS]
+                        sums[rows, g * PTS : (g + 1) * PTS] += row * coef
+
         return 0
 
     lax.fori_loop(0, 2, body, 0)
     total = dot_two(sums[...], summing())
-    for part, out in enumerate((out0, out1, out2, out3)):
+    for part in range(4):
         packed = jnp.zeros((ROWS, PTS), F32)
         for t in range(4):
             at = (part * 4 + t) * ROWS
             packed = jnp.where(segment == t, total[at : at + ROWS], packed)
-        out[...] = packed
-
-
-def near_kernel(place, near, g_left, g_own, g_right, v_left, v_own, v_right, out_ref, geo, weights):
+        out_ref[part] = packed
+
+
+def near_kernel(place, near, left, own, right, out_ref, geo, weights):
     rank, base = place[0], place[2] * OWN - OWN
     zeros = jnp.zeros((PTS, ROWS), BF16)
     for s in range(3 * OWN):
         which, at = divmod(s, OWN)
-        g_ref, v_ref = ((g_left, v_left), (g_own, v_own), (g_right, v_right))[which]
+        ref = (left, own, right)[which]
         cut = slice(at * PTS, (at + 1) * PTS)
-        geo[s, 0:3] = g_ref[0:3, cut]
-        geo[s, 3:6] = g_ref[3:6, cut] * CONTRAST
-        scaled = v_ref[:, cut] * g_ref[6:7, cut]
+        geo[s, 0:3] = ref[ROWS : ROWS + 3, cut]
+        geo[s, 3:6] = ref[ROWS + 3 : ROWS + 6, cut] * CONTRAST
+        scaled = ref[:ROWS, cut] * ref[ROWS + 6 : ROWS + 7, cut]
         high = scaled.astype(BF16).astype(F32)
         turned = jnp.transpose(jnp.concatenate([high, scaled - high], 0)).astype(BF16)
         weights[s, 0:PTS] = turned
@@ -163,10 +169,10 @@
     weights[3 * OWN] = jnp.zeros((2 * PTS, 2 * ROWS), BF16)
 
     def body(i, _):
-        own = jnp.transpose(geo[OWN + i])
-        px = jnp.broadcast_to(own[:, 0:1], (PTS, PTS))
-        py = jnp.broadcast_to(own[:, 1:2], (PTS, PTS))
-        pz = jnp.broadcast_to(own[:, 2:3], (PTS, PTS))
+        at = jnp.transpose(geo[OWN + i])
+        px = jnp.broadcast_to(at[:, 0:1], (PTS, PTS))
+        py = jnp.broadcast_to(at[:, 1:2], (PTS, PTS))
+        pz = jnp.broadcast_to(at[:, 2:3], (PTS, PTS))
         total = jnp.zeros((PTS, 2 * ROWS), F32)
         for j in range(NEAR):
             n = near[rank * OWN + i, j]
@@ -186,14 +192,14 @@
 
 
 def final_kernel(
-    place, lists, part0, part1, part2, part3, left, first, last, right,
+    place, lists, parts, left, own, right,
     one_ref, two_ref, mats_ref, basis_ref, near_ref, out_ref, table, sums, spread, two_rows,
 ):
     rank, base = place[0], place[2] * 8 - 4
     two_rows[...] = own_half(two_ref, rank)
     segment = lane_segment(ROWS)
-    for at, ref in enumerate((left, first, last, right)):
-        table[at] = ref[...]
+    for at, (ref, half) in enumerate(((left, 1), (own, 0), (own, 1), (right, 0))):
+        table[at] = ref[:, half * PTS : (half + 1) * PTS]
 
     for t in range(8):
         acc = [None] * 8
@@ -208,7 +214,7 @@
         for g in range(8):
             sums[t * ROWS : (t + 1) * ROWS, g * PTS : (g + 1) * PTS] = acc[g]
     mid = dot_two(sums[...], summing())
-    down = part0[...] + part1[...] + part2[...] + part3[...]
+    down = parts[0] + parts[1] + parts[2] + parts[3]
     rows = jnp.concatenate([jnp.where(segment == t, down, 0.0) for t in range(4)], 0)
     spread[: 4 * ROWS] = dot_two(rows, spreading(4))
     mids = []
@@ -254,12 +260,7 @@
     up_by_one = [(i, i + 1) for i in range(size - 1)]
     down_by_one = [(i + 1, i) for i in range(size - 1)]
 
-    def both(low, high):
-        return lax.ppermute(high, ALL, up_by_one), lax.ppermute(low, ALL, down_by_one)
-
-    geo_left, geo_right = both(geometry, geometry)
     val = lax.all_to_all(values, "r", split_axis=1, concat_axis=0, tiled=True)
-    val_left, val_right = both(val, val)
 
     def rows_of(height, width):
         return pl.BlockSpec((height, width), lambda i, place: (place[0], 0))
@@ -271,13 +272,13 @@
     transfer_two = transfer_two.reshape(2, 8, 2048)
     couple_two = couple_two.reshape(2, 8, 8192)
 
-    first, last, top = pl.pallas_call(
+    strip, top = pl.pallas_call(
         up_kernel,
         grid_spec=pltpu.PrefetchScalarGridSpec(
             num_scalar_prefetch=1,
             grid=(1,),
-            in_specs=[whole(ROWS, OWN * PTS), whole(OWN, RANK, PTS), rows_of(8, 2048), two_of],
-            out_specs=[whole(ROWS, PTS), whole(ROWS, PTS), whole(gathered, ROWS, PTS)],
+            in_specs=[whole(ROWS, OWN * PTS), whole(7, OWN * PTS), whole(OWN, RANK, PTS), rows_of(8, 2048), two_of],
+            out_specs=[whole(*STRIP), whole(gathered, ROWS, PTS)],
             scratch_shapes=[
                 pltpu.VMEM((OWN, ROWS, PTS), F32),
                 pltpu.VMEM((8 * ROWS, PTS), F32),
@@ -285,31 +286,31 @@
                 pltpu.VMEM((8, 2048), F32),
             ],
         ),
-        out_shape=[shape(ROWS, PTS), shape(ROWS, PTS), shape(gathered, ROWS, PTS)],
+        out_shape=[shape(*STRIP), shape(gathered, ROWS, PTS)],
         compiler_params=PARAMS,
         cost_estimate=pl.CostEstimate(flops=40_000_000, bytes_accessed=600_000, transcendentals=0),
-    )(place, val, basis, transfer_one, transfer_two)
+    )(place, val, geometry, basis, transfer_one, transfer_two)
+
+    left = lax.ppermute(strip, ALL, up_by_one)
+    right = lax.ppermute(strip, ALL, down_by_one)
 
     mine = lax.all_to_all(top, ("x", "z"), split_axis=0, concat_axis=0, tiled=True)
     other = lax.ppermute(mine, "c", [(0, 1), (1, 0)])
-    left, right = both(first, last)
 
     parts = pl.pallas_call(
         couple_kernel,
         in_specs=[SMEM, SMEM, VMEM, VMEM, VMEM],
-        out_specs=[VMEM] * 4,
-        out_shape=[shape(ROWS, PTS)] * 4,
+        out_specs=VMEM,
+        out_shape=shape(4, ROWS, PTS),
         scratch_shapes=[pltpu.VMEM((2 * gathered, ROWS, PTS), F32), pltpu.VMEM((16 * ROWS, 1024), F32)],
         compiler_params=PARAMS,
         cost_estimate=pl.CostEstimate(flops=100_000_000, bytes_accessed=1_000_000, transcendentals=0),
     )(place, lists_two, mine, other, couple_two)
-    received = [parts[0]]
-    for s in range(1, 4):
-        received.append(lax.ppermute(parts[s], "r", [(i, i ^ s) for i in range(4)]))
+    parts = lax.all_to_all(parts, "r", split_axis=0, concat_axis=0, tiled=True)
 
     near_part = pl.pallas_call(
         near_kernel,
-        in_specs=[SMEM, SMEM] + [VMEM] * 6,
+        in_specs=[SMEM, SMEM] + [VMEM] * 3,
         out_specs=VMEM,
         out_shape=shape(ROWS, OWN * PTS),
         scratch_shapes=[
@@ -318,7 +319,7 @@
         ],
         compiler_params=PARAMS,
         cost_estimate=pl.CostEstimate(flops=3_000_000_000, bytes_accessed=700_000, transcendentals=1_600_000),
-    )(place, near, geo_left, geometry, geo_right, val_left, val, val_right)
+    )(place, near, left, strip, right)
 
     result = pl.pallas_call(
         final_kernel,
@@ -326,7 +327,8 @@
             num_scalar_prefetch=1,
             grid=(1,),
             in_specs=[SMEM]
-            + [whole(ROWS, PTS)] * 8
+            + [whole(4, ROWS, PTS)]
+            + [pl.BlockSpec((ROWS, 2 * PTS), lambda i, place: (0, OWN // 2))] * 3
             + [rows_of(8, 2048), two_of, rows_of(8, 8192), whole(OWN, RANK, PTS), whole(ROWS, OWN * PTS)],
             out_specs=whole(ROWS, OWN * PTS),
             scratch_shapes=[
@@ -340,7 +342,7 @@
         compiler_params=PARAMS,
         cost_estimate=pl.CostEstimate(flops=40_000_000, bytes_accessed=1_000_000, transcendentals=0),
     )(
-        place, lists_one, *received, left, first, last, right,
+        place, lists_one, parts, left, strip, right,
         transfer_one, transfer_two, couple_one, basis, near_part,
     )
     return lax.all_to_all(result, "r", split_axis=0, concat_axis=1, tiled=True)

time: 99.6 us -> 80.7 us (0.81)
  starting transfers between devices: 38.8 us -> 17.8 us
  blocking collectives: 30.1 us -> 32.1 us
  Pallas kernels: 21.5 us -> 20.2 us
    ppermute x9 -> x2, starting transfers between devices: 34.2 us -> 9.9 us  [the longest x1 7.31 us: on_device(): right = lax.ppermute(strip, ALL, down_by_one)]
    all_to_all x0 -> x1, starting transfers between devices: none -> 3.26 us  [on_device(): parts = lax.all_to_all(parts, 'r', split_axis=0, concat_axis=0, tiled=True)]
    all_to_all x1, blocking collectives: 8.36 us -> 10.5 us  [on_device(): return lax.all_to_all(result, 'r', split_axis=0, concat_axis=1, tiled=True)]
    pallas_call x1, Pallas kernels: 5.55 us -> 4.25 us  [on_device(): pl.pallas_call(couple_kernel, in_specs=[SMEM, SMEM, VMEM, VMEM, VMEM], ou...]
  transfers between devices with their start and end apart: 11 -> 5, of which waited for: 1 -> 1; matrix products, arithmetic and copies ran while one was open for 0% -> 0% of each run, Pallas kernels for 17% -> 20%
where the time goes in v1:
time: 80.7 us; the launch traced here: 79.6 us
  blocking collectives  32.1 us (40%)
  Pallas kernels  20.2 us (25%)
  starting transfers between devices  17.8 us (22%)
  waiting for transfers between devices  5.91 us (7%)
  local copies, waits for them, and re-layouts  3.38 us (4%)
    all_to_all x1, blocking collectives, on_device(): lax.all_to_all(top, ('x', 'z'), split_axis=0, concat_axis=0, tiled=True)  21.6 us
    pallas_call x1, Pallas kernels, on_device(): pl.pallas_call(near_kernel, in_specs=[SMEM, SMEM] + [VMEM] * 3, out_specs...  11.4 us
    all_to_all x1, blocking collectives, on_device(): return lax.all_to_all(result, 'r', split_axis=0, concat_axis=1, tiled=True)  10.5 us
    ppermute x1, starting transfers between devices, on_device(): right = lax.ppermute(strip, ALL, down_by_one)  7.31 us
    all_to_all x1, waiting for transfers between devices, on_device(): val = lax.all_to_all(values, 'r', split_axis=1, concat_axis=0, tiled=True)  5.9 us
    all_to_all x1, starting transfers between devices, on_device(): val = lax.all_to_all(values, 'r', split_axis=1, concat_axis=0, tiled=True)  4.59 us
    pallas_call x1, Pallas kernels, on_device(): pl.pallas_call(couple_kernel, in_specs=[SMEM, SMEM, VMEM, VMEM, VMEM], ou...  4.25 us
    unnamed x24, local copies, waits for them, and re-layouts  3.29 us
  transfers between devices with their start and end apart: 5, of which 1 were waited for; matrix products, arithmetic and copies ran while one was open for 0% of the time, Pallas kernels for 20%

profile of v1, /device:TPU:2, one launch (start us, length us, event | category | flops | bytes accessed | tf_op | source)
XLA Modules:
  0.0 79.6 jit_solution(10235366642458573297)
XLA Ops:
  0.0 0.0 copy-start
  0.0 0.0 copy-start.1
  0.0 4.6 %all-to-all-start = ((f32[4,4,2048]{2,0,1:T(4,128)}), f32[4,4,2048]{2,0,1:T(4,128)S(1)}, u32[]{:S(2)}, u32[]{:S(2)}) async-start(f32[4,4,2048]{2,0,1:T(4,128)} %bitcast.15), calls=%async_computation | async-start | bytes 262144 | tf_op jit(solution)/shard_map/all_to_all | solution.py:263
  4.6 0.1 pad_add_fusion.place
  4.7 5.9 %all-to-all-done = f32[4,4,2048]{2,0,1:T(4,128)S(1)} async-done(((f32[4,4,2048]{2,0,1:T(4,128)}), f32[4,4,2048]{2,0,1:T(4,128)S(1)}, u32[]{:S(2)}, u32[]{:S(2)}) %all-to-all-start) | async-done | bytes 131104 | tf_op jit(solution)/shard_map/all_to_all | solution.py:263
  10.6 0.0 copy-done
  10.6 0.0 copy-done.1
  10.6 0.0 copy-start.3
  10.7 0.9 %copy-done.3 = f32[16,2048]{1,0:T(8,128)S(1)} copy-done((f32[16,2048]{1,0:T(8,128)S(1)}, f32[16,2048]{1,0:T(8,128)}, u32[]{:S(2)}) %copy-start.3) | copy-done | bytes 131096
  11.6 0.0 copy-start.6
  11.6 0.8 %copy-done.6 = f32[7,2048]{1,0:T(8,128)S(1)} copy-done((f32[7,2048]{1,0:T(8,128)S(1)}, f32[7,2048]{1,0:T(8,128)}, u32[]{:S(2)}) %copy-start.6) | copy-done | bytes 57368
  12.4 0.0 copy-start.5
  12.4 1.4 %shard_map.100 = (f32[24,2304]{1,0:T(8,128)S(1)}, f32[32,16,128]{2,1,0:T(8,128)S(1)}) custom-call(s32[3]{0:T(128)S(1)} %pad_add_fusion.place, f32[16,2048]{1,0:T(8,128)S(1)} %all_to_all.37.v_ref, f32[7,2048]{1,0:T(8,128)S(1)} %copy-done.6, f32[16,32,128]{2,1,0:T(8,128)S(1)} %copy-done, f32[32,2048]{1,0:T(8,128)S(1)} %copy-done.1, f32[2,8,2048]{2,1,0:T(8,128)S(1)} %bitcast.10), custom_call_target="tpu_custom_call" | custom-call | flops 40000000 | bytes 600000 | tf_op jit(solution)/shard_map/pallas_call | solution.py:275
  13.8 0.0 copy-start.7
  13.8 21.6 %all_to_all.48.mine_ref = f32[32,16,128]{2,1,0:T(8,128)S(1)} all-to-all(f32[32,16,128]{2,1,0:T(8,128)S(1)} %get-tuple-element.7), channel_id=1, replica_groups=mesh['x'=4,'z'=8,'c'=2,'r'=4] {'x','z'}, dimensions={0} | all-to-all | bytes 524288 | tf_op jit(solution)/shard_map/all_to_all | solution.py:297
  35.4 0.0 collective-permute-start
  35.4 0.0 copy-start.8
  35.4 2.6 %collective-permute-start.1 = (f32[24,2304]{1,0:T(8,128)S(1)}, f32[24,2304]{1,0:T(8,128)S(1)}, u32[]{:S(2)}, u32[]{:S(2)}) collective-permute-start(f32[24,2304]{1,0:T(8,128)S(1)} %get-tuple-element.8.own), channel_id=1, source_target_pairs={{0,1},{1,2},{2,3},{3,4},{4,5},{5,6},{6,7},{7,8},{8,9},{9,10},{10,1... | collective-permute-start | bytes 663560 | tf_op jit(solution)/shard_map/ppermute | solution.py:294
  38.0 7.3 %collective-permute-start.2 = (f32[24,2304]{1,0:T(8,128)S(1)}, f32[24,2304]{1,0:T(8,128)S(1)}, u32[]{:S(2)}, u32[]{:S(2)}) collective-permute-start(f32[24,2304]{1,0:T(8,128)S(1)} %get-tuple-element.8.own), channel_id=1, source_target_pairs={{1,0},{2,1},{3,2},{4,3},{5,4},{6,5},{7,6},{8,7},{9,8},{10,9},{11,1... | collective-permute-start | bytes 663560 | tf_op jit(solution)/shard_map/ppermute | solution.py:295
  45.4 0.0 copy-done.7
  45.4 0.1 copy.14.lists
  45.4 0.0 copy-done.8
  45.4 0.0 copy-start.9
  45.5 0.1 copy.12.lists
  45.5 0.6 copy-done.9
  46.1 0.1 copy.13.near
  46.2 0.0 collective-permute-done.other_ref
  46.2 0.0 copy-done.5
  46.2 4.3 %shard_map.101 = f32[4,16,128]{2,1,0:T(8,128)} custom-call(s32[3]{0:T(128)S(1)} %pad_add_fusion.place, s32[16,8]{1,0:T(8,128)S(1)} %copy.12.lists, f32[32,16,128]{2,1,0:T(8,128)S(1)} %all_to_all.48.mine_ref, f32[32,16,128]{2,1,0:T(8,128)S(1)} %collective-permute-done.other_ref, f32[2,8,8192]{2,1,0:T(8,128)S(1)} %bitcast.12), custom_call_target="tpu_custom_call" | custom-call | flops 100000000 | bytes 1000000 | tf_op jit(solution)/shard_map/pallas_call | solution.py:300
  50.5 3.3 %all-to-all-start.2 = ((f32[4,16,128]{2,1,0:T(8,128)}), f32[4,16,128]{2,1,0:T(8,128)S(1)}, u32[]{:S(2)}, u32[]{:S(2)}) async-start(f32[4,16,128]{2,1,0:T(8,128)} %shard_map.101), calls=%async_computation.2 | async-start | bytes 65536 | tf_op jit(solution)/shard_map/all_to_all | solution.py:309
  53.8 0.0 copy-start.2
  53.8 0.0 copy-start.4
  53.8 0.0 collective-permute-done.1.left
  53.8 0.0 collective-permute-done.2.right
  53.8 11.4 %shard_map.102.near_ref = f32[16,2048]{1,0:T(8,128)S(1)} custom-call(s32[3]{0:T(128)S(1)} %pad_add_fusion.place, s32[64,6]{1,0:T(8,128)S(1)} %copy.13.near, f32[24,2304]{1,0:T(8,128)S(1)} %collective-permute-done.1.left, f32[24,2304]{1,0:T(8,128)S(1)} %get-tuple-element.8.own, f32[24,2304]{1,0:T(8,128)S(1)} %collective-permute-done.2.right), custom_call_target="tpu_custom_call" | custom-call | flops 3000000000 | bytes 700000 | tf_op jit(solution)/shard_map/pallas_call | solution.py:311
  65.2 0.0 all-to-all-done.2.parts
  65.2 0.0 copy-done.2
  65.2 0.0 copy-done.4
  65.3 3.1 %shard_map.103 = f32[16,2048]{1,0:T(8,128)S(1)} custom-call(s32[3]{0:T(128)S(1)} %pad_add_fusion.place, s32[32,8]{1,0:T(8,128)S(1)} %copy.14.lists, f32[4,16,128]{2,1,0:T(8,128)S(1)} %all-to-all-done.2.parts, f32[24,2304]{1,0:T(8,128)S(1)} %collective-permute-done.1.left, f32[24,2304]{1,0:T(8,128)S(1)} %get-tuple-element.8.own, ...), custom_call_target="tpu_custom_call" | custom-call | flops 40000000 | bytes 1000000 | tf_op jit(solution)/shard_map/pallas_call | solution.py:324
  68.4 10.5 %all_to_all.49 = f32[4,4,2048]{2,1,0:T(4,128)S(1)} all-to-all(f32[4,4,2048]{2,1,0:T(4,128)S(1)} %all_to_all.40), channel_id=1, replica_groups=mesh['x'=4,'z'=8,'c'=2,'r'=4] {'r'}, dimensions={0} | all-to-all | bytes 262144 | tf_op jit(solution)/shard_map/all_to_all | solution.py:348
  78.9 0.7 copy.17
  (2 shorter events, 0.1 us)
Async XLA Ops:
  0.0 10.6 %copy-start = (f32[16,32,128]{2,1,0:T(8,128)S(1)}, f32[16,32,128]{2,1,0:T(8,128)}, u32[]{:S(2)}) copy-start(f32[16,32,128]{2,1,0:T(8,128)} %basis_ref.3) | copy-start | bytes 786436
  0.0 10.6 %copy-start.1 = (f32[32,2048]{1,0:T(8,128)S(1)}, f32[32,2048]{1,0:T(8,128)}, u32[]{:S(2)}) copy-start(f32[32,2048]{1,0:T(8,128)} %one_ref.3) | copy-start | bytes 786436
  0.0 10.6 %all-to-all-start = ((f32[4,4,2048]{2,0,1:T(4,128)}), f32[4,4,2048]{2,0,1:T(4,128)S(1)}, u32[]{:S(2)}, u32[]{:S(2)}) async-start(f32[4,4,2048]{2,0,1:T(4,128)} %bitcast.15), calls=%async_computation | async-start | bytes 262144 | tf_op jit(solution)/shard_map/all_to_all | solution.py:263
  10.6 0.9 %copy-start.3 = (f32[16,2048]{1,0:T(8,128)S(1)}, f32[16,2048]{1,0:T(8,128)}, u32[]{:S(2)}) copy-start(f32[16,2048]{1,0:T(8,128)} %param.15) | copy-start | bytes 393220
  11.6 0.8 %copy-start.6 = (f32[7,2048]{1,0:T(8,128)S(1)}, f32[7,2048]{1,0:T(8,128)}, u32[]{:S(2)}) copy-start(f32[7,2048]{1,0:T(8,128)} %geo_ref.1) | copy-start | bytes 172036
  12.4 33.8 %copy-start.5 = (f32[16,8192]{1,0:T(8,128)S(1)}, f32[16,8192]{1,0:T(8,128)}, u32[]{:S(2)}) copy-start(f32[16,8192]{1,0:T(8,128)} %param.17) | copy-start | bytes 1572868
  13.8 31.5 %copy-start.7 = (s32[32,8]{0,1:T(8,128)S(1)}, s32[32,8]{0,1:T(8,128)}, u32[]{:S(2)}) copy-start(s32[32,8]{0,1:T(8,128)} %param.18) | copy-start | bytes 3076
  35.4 10.8 %collective-permute-start = (f32[32,16,128]{2,1,0:T(8,128)S(1)}, f32[32,16,128]{2,1,0:T(8,128)S(1)}, u32[]{:S(2)}, u32[]{:S(2)}) collective-permute-start(f32[32,16,128]{2,1,0:T(8,128)S(1)} %all_to_all.48.mine_ref), channel_id=1, source_target_pairs={{0,4},{4,0},{1,5},{5,1},{2,6},{6,2},{3,7},{7,3},{8,12},{12,8},{9,1... | collective-permute-start | bytes 786440 | tf_op jit(solution)/shard_map/ppermute | solution.py:298
  35.4 10.0 %copy-start.8 = (s32[16,8]{0,1:T(8,128)S(1)}, s32[16,8]{0,1:T(8,128)}, u32[]{:S(2)}) copy-start(s32[16,8]{0,1:T(8,128)} %param.19) | copy-start | bytes 1540
  35.4 18.4 %collective-permute-start.1 = (f32[24,2304]{1,0:T(8,128)S(1)}, f32[24,2304]{1,0:T(8,128)S(1)}, u32[]{:S(2)}, u32[]{:S(2)}) collective-permute-start(f32[24,2304]{1,0:T(8,128)S(1)} %get-tuple-element.8.own), channel_id=1, source_target_pairs={{0,1},{1,2},{2,3},{3,4},{4,5},{5,6},{6,7},{7,8},{8,9},{9,10},{10,1... | collective-permute-start | bytes 663560 | tf_op jit(solution)/shard_map/ppermute | solution.py:294
  38.0 15.8 %collective-permute-start.2 = (f32[24,2304]{1,0:T(8,128)S(1)}, f32[24,2304]{1,0:T(8,128)S(1)}, u32[]{:S(2)}, u32[]{:S(2)}) collective-permute-start(f32[24,2304]{1,0:T(8,128)S(1)} %get-tuple-element.8.own), channel_id=1, source_target_pairs={{1,0},{2,1},{3,2},{4,3},{5,4},{6,5},{7,6},{8,7},{9,8},{10,9},{11,1... | collective-permute-start | bytes 663560 | tf_op jit(solution)/shard_map/ppermute | solution.py:295
  45.4 0.7 copy-start.9
  50.5 14.7 %all-to-all-start.2 = ((f32[4,16,128]{2,1,0:T(8,128)}), f32[4,16,128]{2,1,0:T(8,128)S(1)}, u32[]{:S(2)}, u32[]{:S(2)}) async-start(f32[4,16,128]{2,1,0:T(8,128)} %shard_map.101), calls=%async_computation.2 | async-start | bytes 65536 | tf_op jit(solution)/shard_map/all_to_all | solution.py:309
  53.8 11.5 %copy-start.2 = (f32[32,8192]{1,0:T(8,128)S(1)}, f32[32,8192]{1,0:T(8,128)}, u32[]{:S(2)}) copy-start(f32[32,8192]{1,0:T(8,128)} %mats_ref.1) | copy-start | bytes 3145732
  53.8 11.5 %copy-start.4 = (f32[16,2048]{1,0:T(8,128)S(1)}, f32[16,2048]{1,0:T(8,128)}, u32[]{:S(2)}) copy-start(f32[16,2048]{1,0:T(8,128)} %param.15) | copy-start | bytes 393220

commit v2 on v1

v2 whole, which is shorter than its diff:
```python
import jax
import jax.numpy as jnp
from jax import lax
from jax.experimental import pallas as pl
from jax.experimental.pallas import tpu as pltpu
from jax.sharding import Mesh
from jax.sharding import PartitionSpec as P

PTS = 128
RANK = 32
NEAR = 6
COUPLE = 8
SOFTEN = 0.05
CONTRAST = 0.6
ROWS = 16
OWN = 16
FIRST = slice(OWN * PTS, OWN * PTS + PTS)
LAST = slice(OWN * PTS + PTS, OWN * PTS + 2 * PTS)
STRIP = (ROWS + 8, OWN * PTS + 2 * PTS)
MESSAGE = OWN * PTS + 2 * PTS + 4 * PTS
F32 = jnp.float32
BF16 = jnp.bfloat16
ALL = ("x", "z", "c", "r")
VMEM = pl.BlockSpec(memory_space=pltpu.VMEM)
ANY = pl.BlockSpec(memory_space=pl.ANY)
SMEM = pl.BlockSpec(memory_space=pltpu.SMEM)
PARAMS = pltpu.CompilerParams(vmem_limit_bytes=40 * 1024 * 1024)


def split(x):
    high = x.astype(BF16)
    return high, (x - high.astype(F32)).astype(BF16)


def dot(a, b):
    return jnp.dot(a, b, preferred_element_type=F32)


def dot_two(x, ones):
    high, low = split(x)
    return dot(high, ones) + dot(low, ones)


def dot_last(a, b):
    return lax.dot_general(a, b, (((1,), (1,)), ((), ())), preferred_element_type=F32)


def lane_segment(rows):
    return lax.broadcasted_iota(jnp.int32, (rows, PTS), 1) >> 5


def fold(x):
    x = x + pltpu.roll(x, 64, 1)
    return x + pltpu.roll(x, 32, 1)


def summing():
    rows = lax.broadcasted_iota(jnp.int32, (1024, PTS), 0) >> 5
    lanes = lax.broadcasted_iota(jnp.int32, (1024, PTS), 1) & 31
    return (rows == lanes).astype(F32).astype(BF16)


def spreading(segments):
    rows = lax.broadcasted_iota(jnp.int32, (PTS, 1024), 0)
    lanes = lax.broadcasted_iota(jnp.int32, (PTS, 1024), 1) >> 5
    return (((rows & 31) == lanes) & (rows < segments * RANK)).astype(F32).astype(BF16)


def pick(packed, segment, slot):
    return fold(jnp.where(segment == slot, packed, 0.0))


def pack(rows, segment):
    packed = rows[:ROWS]
    for t in range(1, 4):
        packed = jnp.where(segment == t, rows[t * ROWS : (t + 1) * ROWS], packed)
    return packed


def up_kernel(
    place, v_ref, geo_hbm, basis_ref, one_hbm, two_hbm, strip_ref, top_ref,
    leaf_c, one_c, sums, geo, one, two, sems,
):
    rank = place[0]
    copies = [
        pltpu.make_async_copy(src, dst, sems.at[at])
        for at, (src, dst) in enumerate(((one_hbm.at[rank], one), (two_hbm.at[rank // 2], two), (geo_hbm, geo)))
    ]
    for copy in copies:
        copy.start()
    segment = lane_segment(ROWS)
    ones = summing()
    zeros = jnp.zeros((2 * RANK, PTS), BF16)
    strip_ref[:ROWS, : OWN * PTS] = v_ref[...]
    for leaf in range(OWN):
        vh, vl = split(v_ref[:, leaf * PTS : (leaf + 1) * PTS])
        bh, bl = split(basis_ref[leaf])
        prod = dot_last(jnp.concatenate([vh, vl], 0), jnp.concatenate([bh, bl, zeros], 0))
        leaf_c[leaf] = fold(prod[:ROWS] + prod[ROWS:])
    copies[0].wait()
    for t in range(8):
        for g in range(8):
            low, high = slice(g * PTS, (g + 1) * PTS), slice(1024 + g * PTS, 1024 + (g + 1) * PTS)
            sums[t * ROWS : (t + 1) * ROWS, low] = (
                one[t : t + 1, low] * leaf_c[2 * t] + one[t : t + 1, high] * leaf_c[2 * t + 1]
            )
    one_c[...] = dot_two(sums[...], ones)
    strip_ref[:ROWS, FIRST] = pack(one_c[: 4 * ROWS], segment)
    strip_ref[:ROWS, LAST] = pack(one_c[4 * ROWS :], segment)
    copies[1].wait()
    two[...] = pltpu.roll(two[...], (rank % 2) * 4, 0)
    for t in range(4):
        for g in range(8):
            low, high = slice(g * PTS, (g + 1) * PTS), slice(1024 + g * PTS, 1024 + (g + 1) * PTS)
            sums[t * ROWS : (t + 1) * ROWS, low] = (
                two[t : t + 1, low] * one_c[2 * t * ROWS : (2 * t + 1) * ROWS]
                + two[t : t + 1, high] * one_c[(2 * t + 1) * ROWS : (2 * t + 2) * ROWS]
            )
    top = pack(dot_two(sums[: 4 * ROWS], ones), segment)
    for copy in range(top_ref.shape[0]):
        top_ref[copy] = top
    copies[2].wait()
    strip_ref[ROWS : ROWS + 7, : OWN * PTS] = geo[...]


def couple_rows(coefs, first, row_of, sums):
    for t in range(sums.shape[0] // ROWS):
        acc = [None] * 8
        for j in range(COUPLE):
            coef = coefs[first + t * COUPLE + j]
            for g in range(8):
                term = row_of(t, slice(j * 1024 + g * PTS, j * 1024 + (g + 1) * PTS)) * coef
                acc[g] = term if j == 0 else acc[g] + term
        for g in range(8):
            sums[t * ROWS : (t + 1) * ROWS, g * PTS : (g + 1) * PTS] = acc[g]


def couple_kernel(place, lists, mine_ref, other_ref, mats_ref, near_ref, out_ref, table, coefs, sums):
    rank, core = place[0], place[1]
    segment = lane_segment(ROWS)
    half = mine_ref.shape[0]
    table[:half] = mine_ref[...]
    table[half:] = other_ref[...]
    for t in range(16):
        for j in range(COUPLE):
            n = lists[t, j]
            live = (n >= 0) & (((n >> 2) & 3) == rank)
            group = jnp.where(live, n >> 4, 0)
            slot = jnp.where(live, n & 3, -1)
            coefs[t * COUPLE + j] = pick(table[((group & 1) ^ core) * half + (group >> 1)], segment, slot)
    couple_rows(coefs, 0, lambda t, lanes: mats_ref[t : t + 1, lanes], sums)
    total = dot_two(sums[...], summing())
    out_ref[:, : OWN * PTS + 2 * PTS] = near_ref[...]
    for part in range(4):
        at = OWN * PTS + (2 + part) * PTS
        out_ref[:, at : at + PTS] = pack(total[part * 4 * ROWS : (part + 1) * 4 * ROWS], segment)


def near_kernel(
    place, near, lists, left, own, right, mats_hbm, out_ref, geo, weights, mats, table, coefs, sums, sem
):
    rank, base = place[0], place[2] * OWN - OWN
    copy = pltpu.make_async_copy(mats_hbm.at[rank], mats, sem)
    copy.start()
    zeros = jnp.zeros((ROWS, PTS), BF16)
    for s in range(3 * OWN):
        which, at = divmod(s, OWN)
        ref = (left, own, right)[which]
        cut = slice(at * PTS, (at + 1) * PTS)
        geo[s, 0:3] = ref[ROWS : ROWS + 3, cut]
        geo[s, 3:6] = ref[ROWS + 3 : ROWS + 6, cut] * CONTRAST
        high, low = split(ref[:ROWS, cut] * ref[ROWS + 6 : ROWS + 7, cut])
        weights[s, :ROWS, :PTS] = high
        weights[s, :ROWS, PTS:] = high
        weights[s, ROWS:, :PTS] = low
        weights[s, ROWS:, PTS:] = zeros
    geo[3 * OWN] = jnp.zeros((8, PTS), F32)
    weights[3 * OWN] = jnp.zeros((2 * ROWS, 2 * PTS), BF16)

    def leaf(i):
        at = jnp.transpose(geo[OWN + i])
        px, py, pz = (jnp.broadcast_to(at[:, k : k + 1], (PTS, PTS)) for k in range(3))
        total = None
        for j in range(NEAR):
            n = near[rank * OWN + i, j]
            s = jnp.where(n >= 0, jnp.clip(n - base, 0, 3 * OWN - 1), 3 * OWN)
            src = geo[s]
            dx, dy, dz = px - src[0:1], py - src[1:2], pz - src[2:3]
            inv = lax.rsqrt(dx * dx + dy * dy + dz * dz + SOFTEN)
            turn = dx * src[3:4] + dy * src[4:5] + dz * src[5:6]
            high, low = split(inv + turn * (inv * inv * inv))
            term = dot_last(jnp.concatenate([high, low], 1), weights[s])
            total = term if j == 0 else total + term
        flat = jnp.transpose(total)
        out_ref[:, pl.ds(pl.multiple_of(i * PTS, PTS), PTS)] = flat[:ROWS] + flat[ROWS:]

    def leaves(step, _):
        for u in range(8):
            leaf(step * 8 + u)
        return 0

    lax.fori_loop(0, OWN // 8, leaves, 0)

    segment = lane_segment(ROWS)
    for at, (ref, lanes) in enumerate(((left, LAST), (own, FIRST), (own, LAST), (right, FIRST))):
        table[at] = ref[:ROWS, lanes]
    first = place[2] * 8 - 4
    for t in range(8):
        for j in range(COUPLE):
            n = lists[rank * 8 + t, j]
            q = jnp.clip(n - first, 0, 15)
            coefs[t * COUPLE + j] = pick(table[q >> 2], segment, jnp.where(n >= 0, q & 3, -1))
    copy.wait()
    couple_rows(coefs, 0, lambda t, lanes: mats[t : t + 1, lanes], sums)
    total = dot_two(sums[...], summing())
    for part in range(2):
        at = OWN * PTS + part * PTS
        out_ref[:, at : at + PTS] = pack(total[part * 4 * ROWS : (part + 1) * 4 * ROWS], segment)


def final_kernel(got, one_ref, two_ref, basis_ref, out_ref, spread_two, spread_one):
    segment = lane_segment(8)
    lower = lax.broadcasted_iota(jnp.int32, (8, PTS), 0) < 4

    def twice(x):
        return jnp.concatenate([x, x], 0)

    def rows_of(ref, t, u, lanes):
        return jnp.where(lower, ref[t : t + 1, lanes], ref[u : u + 1, lanes])

    def apply(ref, t, u, k, spread, at):
        acc = None
        for g in range(8):
            rows = rows_of(ref, t, u, slice(k * 1024 + g * PTS, k * 1024 + (g + 1) * PTS))
            term = rows * spread[at : at + 8, g * PTS : (g + 1) * PTS]
            acc = term if g == 0 else acc + term
        return acc

    start = OWN * PTS + 2 * PTS
    rows = []
    for part in range(4):
        lanes = slice(start + part * PTS, start + (part + 1) * PTS)
        down = twice(got[0, :, lanes] + got[1, :, lanes] + got[2, :, lanes] + got[3, :, lanes])
        for slot in (0, 2):
            rows.append(jnp.where(segment == jnp.where(lower, slot, slot + 1), down, 0.0))
    spread_two[...] = dot_two(jnp.concatenate(rows, 0), spreading(4))
    mids = []
    for m in range(8):
        lanes = slice(OWN * PTS + (m % 2) * PTS, OWN * PTS + (m % 2 + 1) * PTS)
        own = twice(got[m // 2, :, lanes])
        for k in range(2):
            acc = apply(two_ref, 2 * m, 2 * m + 1, k, spread_two, 8 * m)
            mids.append(fold(acc + jnp.where(segment == jnp.where(lower, k, k + 2), own, 0.0)))
    spread_one[...] = dot_two(jnp.concatenate(mids, 0), spreading(1))
    zeros = jnp.zeros((RANK, PTS), BF16)
    for m in range(8):
        for k in range(2):
            t, u = 4 * m + k, 4 * m + k + 2
            for side in range(2):
                down = fold(apply(one_ref, t, u, side, spread_one, (2 * m + k) * 8))
                high = down.astype(BF16).astype(F32)
                lhs = jnp.where(segment == 1, down - high, jnp.where(segment == 3, 0.0, high)).astype(BF16)
                pair = []
                for leaf in (2 * t + side, 2 * u + side):
                    bh, bl = split(basis_ref[leaf])
                    pair.append(jnp.concatenate([bh, bh, bl, zeros], 0))
                far = dot(lhs, jnp.concatenate(pair, 1))
                for leaf, part in ((2 * t + side, far[:4, :PTS]), (2 * u + side, far[4:, PTS:])):
                    at = leaf % OWN * PTS
                    out_ref[:, leaf * PTS : (leaf + 1) * PTS] = got[leaf // OWN, :, at : at + PTS] + part


def shape(*dims):
    return jax.ShapeDtypeStruct(dims, F32)


def scratch(*dims):
    return pltpu.VMEM(dims, F32)


def on_device(values, geometry, basis, near, transfer_one, transfer_two, couple_one, couple_two, lists_one, lists_two):
    size = lax.axis_size("x") * lax.axis_size("z") * lax.axis_size("c") * lax.axis_size("r")
    gathered = lax.axis_size("x") * lax.axis_size("z")
    place = jnp.stack([lax.axis_index("r"), lax.axis_index("c"), lax.axis_index(ALL)]).astype(jnp.int32)

    basis_all = lax.all_gather(basis, "r", axis=0, tiled=True)
    val = lax.all_to_all(values, "r", split_axis=1, concat_axis=0, tiled=True)
    strip, top = pl.pallas_call(
        up_kernel,
        in_specs=[SMEM, VMEM, ANY, VMEM, ANY, ANY],
        out_specs=[VMEM, VMEM],
        out_shape=[shape(*STRIP), shape(gathered, ROWS, PTS)],
        scratch_shapes=[
            scratch(OWN, ROWS, PTS),
            scratch(8 * ROWS, PTS),
            scratch(8 * ROWS, 1024),
            scratch(7, OWN * PTS),
            scratch(8, 2048),
            scratch(8, 2048),
            pltpu.SemaphoreType.DMA((3,)),
        ],
        compiler_params=PARAMS,
        cost_estimate=pl.CostEstimate(flops=40_000_000, bytes_accessed=600_000, transcendentals=0),
    )(place, val, geometry, basis, transfer_one.reshape(4, 8, 2048), transfer_two.reshape(2, 8, 2048))

    left = lax.ppermute(strip, ALL, [(i, i + 1) for i in range(size - 1)])
    right = lax.ppermute(strip, ALL, [(i + 1, i) for i in range(size - 1)])
    mine = lax.all_to_all(top, ("x", "z"), split_axis=0, concat_axis=0, tiled=True)
    other = lax.ppermute(mine, "c", [(0, 1), (1, 0)])

    near_part = pl.pallas_call(
        near_kernel,
        in_specs=[SMEM, SMEM, SMEM, VMEM, VMEM, VMEM, ANY],
        out_specs=VMEM,
        out_shape=shape(ROWS, OWN * PTS + 2 * PTS),
        scratch_shapes=[
            scratch(3 * OWN + 1, 8, PTS),
            pltpu.VMEM((3 * OWN + 1, 2 * ROWS, 2 * PTS), BF16),
            scratch(8, 8192),
            scratch(4, ROWS, PTS),
            scratch(8 * COUPLE, ROWS, PTS),
            scratch(8 * ROWS, 1024),
            pltpu.SemaphoreType.DMA(()),
        ],
        compiler_params=PARAMS,
        cost_estimate=pl.CostEstimate(flops=3_000_000_000, bytes_accessed=700_000, transcendentals=1_600_000),
    )(place, near, lists_one, left, strip, right, couple_one.reshape(4, 8, 8192))

    message = pl.pallas_call(
        couple_kernel,
        in_specs=[SMEM, SMEM, VMEM, VMEM, VMEM, VMEM],
        out_specs=VMEM,
        out_shape=shape(ROWS, MESSAGE),
        scratch_shapes=[
            scratch(2 * gathered, ROWS, PTS),
            scratch(16 * COUPLE, ROWS, PTS),
            scratch(16 * ROWS, 1024),
        ],
        compiler_params=PARAMS,
        cost_estimate=pl.CostEstimate(flops=100_000_000, bytes_accessed=1_000_000, transcendentals=0),
    )(place, lists_two, mine, other, couple_two, near_part)
    got = lax.all_to_all(message.reshape(4, 4, MESSAGE), "r", split_axis=0, concat_axis=0, tiled=True)

    return pl.pallas_call(
        final_kernel,
        in_specs=[VMEM] * 4,
        out_specs=VMEM,
        out_shape=shape(4, 4 * OWN * PTS),
        scratch_shapes=[scratch(64, 1024), scratch(128, 1024)],
        compiler_params=PARAMS,
        cost_estimate=pl.CostEstimate(flops=40_000_000, bytes_accessed=2_000_000, transcendentals=0),
    )(got, transfer_one, transfer_two, basis_all)


def solution(mesh):
    fine = Mesh(mesh.devices.reshape(4, 8, 2, 4), ALL)
    leaf = ("x", "z", "c")
    return jax.shard_map(
        on_device,
        mesh=fine,
        in_specs=(
            P("r", leaf),
            P(None, ALL),
            P(ALL, None, None),
            P(leaf, None),
            P(leaf, None),
            P(leaf, None),
            P(leaf, None),
            P(leaf, None),
            P(leaf, None),
            P(leaf, None),
        ),
        out_specs=P("r", leaf),
        check_vma=False,
    )
```

time: 80.7 us -> 77.6 us (0.962)
  blocking collectives: 32.1 us -> 9.35 us
  between operations: 0.15 us -> 13.6 us
  starting transfers between devices: 17.8 us -> 26 us
  Pallas kernels: 20.2 us -> 16.5 us
  waiting for transfers between devices: 5.91 us -> 9.17 us
  local copies, waits for them, and re-layouts: 3.38 us -> 2.21 us
    all_to_all x2 -> x1, blocking collectives: 32.1 us -> 9.35 us  [on_device(): lax.all_to_all(message.reshape(4, 4, MESSAGE), 'r', split_axis=0, concat_...]
    all_to_all x1, starting transfers between devices: 3.26 us -> 11.6 us  [on_device(): lax.all_to_all(top, ('x', 'z'), split_axis=0, concat_axis=0, tiled=True)]
    pallas_call x4, Pallas kernels: 20.2 us -> 16.5 us  [the longest x1 9.84 us: on_device(): pl.pallas_call(near_kernel, in_specs=[SMEM, SMEM, SMEM, VMEM, VMEM, VMEM,...]
    ppermute x2, waiting for transfers between devices: 0.01 us -> 2.55 us  [the longest x1 1.5 us: on_device(): right = lax.ppermute(strip, ALL, [(i + 1, i) for i in range(size - 1)])]
    unnamed x24 -> x23, local copies, waits for them, and re-layouts: 3.29 us -> 2.11 us
  transfers between devices with their start and end apart: 5 -> 6, of which waited for: 1 -> 3; matrix products, arithmetic and copies ran while one was open for 0% -> 0% of each run, Pallas kernels for 20% -> 19%
where the time goes in v2:
time: 77.6 us; the launch traced here: 76.8 us
  starting transfers between devices  26 us (34%)
  Pallas kernels  16.5 us (21%)
  between operations  13.6 us (18%)
  blocking collectives  9.35 us (12%)
  waiting for transfers between devices  9.17 us (12%)
  local copies, waits for them, and re-layouts  2.21 us (3%)
    all_to_all x1, starting transfers between devices, on_device(): lax.all_to_all(top, ('x', 'z'), split_axis=0, concat_axis=0, tiled=True)  11.6 us
    pallas_call x1, Pallas kernels, on_device(): pl.pallas_call(near_kernel, in_specs=[SMEM, SMEM, SMEM, VMEM, VMEM, VMEM,...  9.84 us
    all_to_all x1, blocking collectives, on_device(): lax.all_to_all(message.reshape(4, 4, MESSAGE), 'r', split_axis=0, concat_...  9.35 us
    ppermute x1, starting transfers between devices, on_device(): right = lax.ppermute(strip, ALL, [(i + 1, i) for i in range(size - 1)])  7.31 us
    all_to_all x1, waiting for transfers between devices, on_device(): val = lax.all_to_all(values, 'r', split_axis=1, concat_axis=0, tiled=True)  5.9 us
    all_to_all x1, starting transfers between devices, on_device(): val = lax.all_to_all(values, 'r', split_axis=1, concat_axis=0, tiled=True)  4.61 us
    pallas_call x1, Pallas kernels, on_device(): pl.pallas_call(up_kernel, in_specs=[SMEM, VMEM, ANY, VMEM, ANY, ANY], out...  2.58 us
    ppermute x1, starting transfers between devices, on_device(): left = lax.ppermute(strip, ALL, [(i, i + 1) for i in range(size - 1)])  2.47 us
  transfers between devices with their start and end apart: 6, of which 3 were waited for; matrix products, arithmetic and copies ran while one was open for 0% of the time, Pallas kernels for 19%

profile of v2, /device:TPU:2, one launch (start us, length us, event | category | flops | bytes accessed | tf_op | source)
XLA Modules:
  0.0 76.8 jit_solution(1308007517086260157)
XLA Ops:
  6.5 0.0 all-gather.2.cloned.1.call-start
  6.5 0.0 copy-start.4
  6.5 0.0 copy-start.5
  6.5 0.7 all-gather.2.cloned.1.call-update
  7.3 0.0 copy-start
  7.3 0.0 copy-start.2
  7.3 0.0 copy-start.6
  7.3 4.6 %all-to-all-start = ((f32[4,4,2048]{2,0,1:T(4,128)}), f32[4,4,2048]{2,0,1:T(4,128)S(1)}, u32[]{:S(2)}, u32[]{:S(2)}) async-start(f32[4,4,2048]{2,0,1:T(4,128)} %bitcast.12), calls=%async_computation | async-start | bytes 262144 | tf_op jit(solution)/shard_map/all_to_all | solution.py:287
  11.9 0.1 pad_add_fusion.place
  12.0 5.9 %all-to-all-done = f32[4,4,2048]{2,0,1:T(4,128)S(1)} async-done(((f32[4,4,2048]{2,0,1:T(4,128)}), f32[4,4,2048]{2,0,1:T(4,128)S(1)}, u32[]{:S(2)}, u32[]{:S(2)}) %all-to-all-start) | async-done | bytes 131104 | tf_op jit(solution)/shard_map/all_to_all | solution.py:287
  17.9 0.0 copy-done.4
  17.9 0.0 copy-done.5
  17.9 0.0 copy-done
  17.9 0.0 copy-done.2
  18.0 2.6 %shard_map.100 = (f32[24,2304]{1,0:T(8,128)S(1)}, f32[32,16,128]{2,1,0:T(8,128)}) custom-call(s32[3]{0:T(128)S(1)} %pad_add_fusion.place, f32[16,2048]{1,0:T(8,128)S(1)} %all_to_all.23.v_ref, f32[7,2048]{1,0:T(8,128)S(1)} %copy-done.5, f32[16,32,128]{2,1,0:T(8,128)S(1)} %copy-done, f32[4,8,2048]{2,1,0:T(8,128)S(1)} %bitcast.8, f32[2,8,2048]{2,1,0:T(8,128)S(1)} %bitcast.9), custom_call_target="tpu_custom_call" | custom-call | flops 40000000 | bytes 600000 | tf_op jit(solution)/shard_map/pallas_call | solution.py:288
  20.5 0.0 copy-start.7
  20.6 11.6 %all-to-all-start.1 = ((f32[32,16,128]{2,1,0:T(8,128)}), f32[32,16,128]{2,1,0:T(8,128)S(1)}, u32[]{:S(2)}, u32[]{:S(2)}) async-start(f32[32,16,128]{2,1,0:T(8,128)} %get-tuple-element.7), calls=%async_computation.1 | async-start | bytes 524288 | tf_op jit(solution)/shard_map/all_to_all | solution.py:308
  32.2 0.0 copy-start.8
  32.2 2.5 %collective-permute-start.1 = (f32[24,2304]{1,0:T(8,128)S(1)}, f32[24,2304]{1,0:T(8,128)S(1)}, u32[]{:S(2)}, u32[]{:S(2)}) collective-permute-start(f32[24,2304]{1,0:T(8,128)S(1)} %get-tuple-element.8.own), channel_id=1, source_target_pairs={{0,1},{1,2},{2,3},{3,4},{4,5},{5,6},{6,7},{7,8},{8,9},{9,10},{10,1... | collective-permute-start | bytes 663560 | tf_op jit(solution)/shard_map/ppermute | solution.py:306
  34.7 7.3 %collective-permute-start.2 = (f32[24,2304]{1,0:T(8,128)S(1)}, f32[24,2304]{1,0:T(8,128)S(1)}, u32[]{:S(2)}, u32[]{:S(2)}) collective-permute-start(f32[24,2304]{1,0:T(8,128)S(1)} %get-tuple-element.8.own), channel_id=1, source_target_pairs={{1,0},{2,1},{3,2},{4,3},{5,4},{6,5},{7,6},{8,7},{9,8},{10,9},{11,1... | collective-permute-start | bytes 663560 | tf_op jit(solution)/shard_map/ppermute | solution.py:307
  42.0 0.0 copy-done.7
  42.0 0.1 copy.16.near
  42.1 0.0 copy-done.8
  42.1 0.0 copy-start.9
  42.1 0.1 copy.17.lists
  42.2 0.6 copy-done.9
  42.8 0.1 copy.18.lists
  42.9 0.0 all-to-all-done.1.mine_ref
  42.9 0.0 collective-permute-start
  42.9 1.0 %collective-permute-done.1.left = f32[24,2304]{1,0:T(8,128)S(1)} collective-permute-done((f32[24,2304]{1,0:T(8,128)S(1)}, f32[24,2304]{1,0:T(8,128)S(1)}, u32[]{:S(2)}, u32[]{:S(2)}) %collective-permute-start.1) | collective-permute-done | bytes 221216 | tf_op jit(solution)/shard_map/ppermute | solution.py:306
  43.9 1.5 %collective-permute-done.2.right = f32[24,2304]{1,0:T(8,128)S(1)} collective-permute-done((f32[24,2304]{1,0:T(8,128)S(1)}, f32[24,2304]{1,0:T(8,128)S(1)}, u32[]{:S(2)}, u32[]{:S(2)}) %collective-permute-start.2) | collective-permute-done | bytes 221216 | tf_op jit(solution)/shard_map/ppermute | solution.py:307
  45.4 0.0 copy-done.6
  45.4 0.0 copy-start.3
  45.4 9.8 %shard_map.101.near_ref = f32[16,2304]{1,0:T(8,128)S(1)} custom-call(s32[3]{0:T(128)S(1)} %pad_add_fusion.place, s32[64,6]{1,0:T(8,128)S(1)} %copy.16.near, s32[32,8]{1,0:T(8,128)S(1)} %copy.17.lists, f32[24,2304]{1,0:T(8,128)S(1)} %collective-permute-done.1.left, f32[24,2304]{1,0:T(8,128)S(1)} %get-tuple-element.8.own, ...), custom_call_target="tpu_custom_call" | custom-call | flops 3000000000 | bytes 700000 | tf_op jit(solution)/shard_map/pallas_call | solution.py:311
  55.3 0.0 collective-permute-done.other_ref
  55.3 0.0 copy-done.3
  55.3 2.1 %shard_map.102 = f32[16,2816]{1,0:T(8,128)S(1)} custom-call(s32[3]{0:T(128)S(1)} %pad_add_fusion.place, s32[16,8]{1,0:T(8,128)S(1)} %copy.18.lists, f32[32,16,128]{2,1,0:T(8,128)S(1)} %all-to-all-done.1.mine_ref, f32[32,16,128]{2,1,0:T(8,128)S(1)} %collective-permute-done.other_ref, f32[16,8192]{1,0:T(8,128)S(1)} %copy-done.3, ...), custom_call_target="tpu_custom_call" | custom-call | flops 100000000 | bytes 1000000 | tf_op jit(solution)/shard_map/pallas_call | solution.py:329
  57.4 0.1 reshape.18
  57.5 9.4 %all_to_all.29.got = f32[4,4,2816]{2,1,0:T(4,128)S(1)} all-to-all(f32[4,4,2816]{2,1,0:T(4,128)S(1)} %reshape.18), channel_id=1, replica_groups=mesh['x'=4,'z'=8,'c'=2,'r'=4] {'r'}, dimensions={0} | all-to-all | bytes 360448 | tf_op jit(solution)/shard_map/all_to_all | solution.py:342
  66.8 0.0 all-gather.2.cloned.1.call-done.basis_ref
  66.8 0.0 copy-start.1
  66.9 1.2 %copy-done.1 = f32[64,32,128]{2,1,0:T(8,128)S(1)} copy-done((f32[64,32,128]{2,1,0:T(8,128)S(1)}, f32[64,32,128]{2,1,0:T(8,128)}, u32[]{:S(2)}) %copy-start.1) | copy-done | bytes 1048600
  68.1 1.9 %shard_map.103 = f32[4,8192]{1,0:T(4,128)} custom-call(f32[4,4,2816]{2,1,0:T(4,128)S(1)} %all_to_all.29.got, f32[32,2048]{1,0:T(8,128)S(1)} %copy-done.2, f32[16,2048]{1,0:T(8,128)S(1)} %copy-done.4, f32[64,32,128]{2,1,0:T(8,128)S(1)} %copy-done.1), custom_call_target="tpu_custom_call" | custom-call | flops 40000000 | bytes 2000000 | tf_op jit(solution)/shard_map/pallas_call | solution.py:344
  (1 shorter events, 0.0 us)
Async XLA Ops:
  6.5 60.3 %all-gather.2.cloned.1.call-start = ((), (), s32[]{:S(2)}) async-start(), calls=%async_computation.3 | async-start | bytes 1310720 | tf_op jit(solution)/shard_map/all_gather | solution.py:286
  6.5 11.4 %copy-start.4 = (f32[16,2048]{1,0:T(8,128)S(1)}, f32[16,2048]{1,0:T(8,128)}, u32[]{:S(2)}) copy-start(f32[16,2048]{1,0:T(8,128)} %two_ref.1) | copy-start | bytes 393220
  6.5 11.4 %copy-start.5 = (f32[7,2048]{1,0:T(8,128)S(1)}, f32[7,2048]{1,0:T(8,128)}, u32[]{:S(2)}) copy-start(f32[7,2048]{1,0:T(8,128)} %geo_hbm.1) | copy-start | bytes 172036
  7.3 10.7 %copy-start = (f32[16,32,128]{2,1,0:T(8,128)S(1)}, f32[16,32,128]{2,1,0:T(8,128)}, u32[]{:S(2)}) copy-start(f32[16,32,128]{2,1,0:T(8,128)} %basis_ref.1) | copy-start | bytes 786436
  7.3 10.7 %copy-start.2 = (f32[32,2048]{1,0:T(8,128)S(1)}, f32[32,2048]{1,0:T(8,128)}, u32[]{:S(2)}) copy-start(f32[32,2048]{1,0:T(8,128)} %one_ref.1) | copy-start | bytes 786436
  7.3 38.2 %copy-start.6 = (f32[32,8192]{1,0:T(8,128)S(1)}, f32[32,8192]{1,0:T(8,128)}, u32[]{:S(2)}) copy-start(f32[32,8192]{1,0:T(8,128)} %param.16) | copy-start | bytes 3145732
  7.3 10.6 %all-to-all-start = ((f32[4,4,2048]{2,0,1:T(4,128)}), f32[4,4,2048]{2,0,1:T(4,128)S(1)}, u32[]{:S(2)}, u32[]{:S(2)}) async-start(f32[4,4,2048]{2,0,1:T(4,128)} %bitcast.12), calls=%async_computation | async-start | bytes 262144 | tf_op jit(solution)/shard_map/all_to_all | solution.py:287
  20.5 21.5 %copy-start.7 = (s32[64,6]{0,1:T(8,128)S(1)}, s32[64,6]{0,1:T(8,128)}, u32[]{:S(2)}) copy-start(s32[64,6]{0,1:T(8,128)} %param.13) | copy-start | bytes 4612
  20.6 22.3 %all-to-all-start.1 = ((f32[32,16,128]{2,1,0:T(8,128)}), f32[32,16,128]{2,1,0:T(8,128)S(1)}, u32[]{:S(2)}, u32[]{:S(2)}) async-start(f32[32,16,128]{2,1,0:T(8,128)} %get-tuple-element.7), calls=%async_computation.1 | async-start | bytes 524288 | tf_op jit(solution)/shard_map/all_to_all | solution.py:308
  32.2 9.9 %copy-start.8 = (s32[32,8]{0,1:T(8,128)S(1)}, s32[32,8]{0,1:T(8,128)}, u32[]{:S(2)}) copy-start(s32[32,8]{0,1:T(8,128)} %param.18) | copy-start | bytes 3076
  32.2 11.7 %collective-permute-start.1 = (f32[24,2304]{1,0:T(8,128)S(1)}, f32[24,2304]{1,0:T(8,128)S(1)}, u32[]{:S(2)}, u32[]{:S(2)}) collective-permute-start(f32[24,2304]{1,0:T(8,128)S(1)} %get-tuple-element.8.own), channel_id=1, source_target_pairs={{0,1},{1,2},{2,3},{3,4},{4,5},{5,6},{6,7},{7,8},{8,9},{9,10},{10,1... | collective-permute-start | bytes 663560 | tf_op jit(solution)/shard_map/ppermute | solution.py:306
  34.7 10.7 %collective-permute-start.2 = (f32[24,2304]{1,0:T(8,128)S(1)}, f32[24,2304]{1,0:T(8,128)S(1)}, u32[]{:S(2)}, u32[]{:S(2)}) collective-permute-start(f32[24,2304]{1,0:T(8,128)S(1)} %get-tuple-element.8.own), channel_id=1, source_target_pairs={{1,0},{2,1},{3,2},{4,3},{5,4},{6,5},{7,6},{8,7},{9,8},{10,9},{11,1... | collective-permute-start | bytes 663560 | tf_op jit(solution)/shard_map/ppermute | solution.py:307
  42.1 0.7 copy-start.9
  42.9 12.4 %collective-permute-start = (f32[32,16,128]{2,1,0:T(8,128)S(1)}, f32[32,16,128]{2,1,0:T(8,128)S(1)}, u32[]{:S(2)}, u32[]{:S(2)}) collective-permute-start(f32[32,16,128]{2,1,0:T(8,128)S(1)} %all-to-all-done.1.mine_ref), channel_id=1, source_target_pairs={{0,4},{4,0},{1,5},{5,1},{2,6},{6,2},{3,7},{7,3},{8,12},{12,8},{9,1... | collective-permute-start | bytes 786440 | tf_op jit(solution)/shard_map/ppermute | solution.py:309
  45.4 9.9 %copy-start.3 = (f32[16,8192]{1,0:T(8,128)S(1)}, f32[16,8192]{1,0:T(8,128)}, u32[]{:S(2)}) copy-start(f32[16,8192]{1,0:T(8,128)} %mats_ref.1) | copy-start | bytes 1572868
  66.8 1.2 %copy-start.1 = (f32[64,32,128]{2,1,0:T(8,128)S(1)}, f32[64,32,128]{2,1,0:T(8,128)}, u32[]{:S(2)}) copy-start(f32[64,32,128]{2,1,0:T(8,128)} %all-gather.2.cloned.1.call-done.basis_ref) | copy-start | bytes 3145732
Sparse Core Ops, SparseCore 0:
  9.2 30.1 all-gather.1

commit v3 on v2

--- a/solution.py
+++ b/solution.py
@@ -22,9 +22,9 @@
 BF16 = jnp.bfloat16
 ALL = ("x", "z", "c", "r")
 VMEM = pl.BlockSpec(memory_space=pltpu.VMEM)
-ANY = pl.BlockSpec(memory_space=pl.ANY)
+HBM = pl.BlockSpec(memory_space=pltpu.HBM)
 SMEM = pl.BlockSpec(memory_space=pltpu.SMEM)
-PARAMS = pltpu.CompilerParams(vmem_limit_bytes=40 * 1024 * 1024)
+PARAMS = pltpu.CompilerParams(vmem_limit_bytes=16 * 1024 * 1024)
 
 
 def split(x):
@@ -77,17 +77,29 @@
     return packed
 
 
-def up_kernel(
-    place, v_ref, geo_hbm, basis_ref, one_hbm, two_hbm, strip_ref, top_ref,
-    leaf_c, one_c, sums, geo, one, two, sems,
-):
+def block(px, py, pz, src):
+    dx, dy, dz = px - src[0:1], py - src[1:2], pz - src[2:3]
+    inv = lax.rsqrt(dx * dx + dy * dy + dz * dz + SOFTEN)
+    turn = dx * src[3:4] + dy * src[4:5] + dz * src[5:6]
+    high, low = split(inv + turn * (inv * inv * inv))
+    return jnp.concatenate([high, low], 1)
+
+
+def prepare_kernel(place, geo_hbm, two_hbm, geo_ref, two_ref, sems):
     rank = place[0]
     copies = [
-        pltpu.make_async_copy(src, dst, sems.at[at])
-        for at, (src, dst) in enumerate(((one_hbm.at[rank], one), (two_hbm.at[rank // 2], two), (geo_hbm, geo)))
+        pltpu.make_async_copy(geo_hbm, geo_ref.at[pl.ds(0, 7)], sems.at[0]),
+        pltpu.make_async_copy(two_hbm.at[rank // 2], two_ref, sems.at[1]),
     ]
     for copy in copies:
         copy.start()
+    for copy in copies:
+        copy.wait()
+    two_ref[...] = pltpu.roll(two_ref[...], (rank % 2) * 4, 0)
+
+
+def up_kernel(place, v_ref, geo_ref, basis_ref, one_ref, two, strip_ref, top_ref, leaf_c, one_c, sums):
+    rank = place[0]
     segment = lane_segment(ROWS)
     ones = summing()
     zeros = jnp.zeros((2 * RANK, PTS), BF16)
@@ -97,18 +109,15 @@
         bh, bl = split(basis_ref[leaf])
         prod = dot_last(jnp.concatenate([vh, vl], 0), jnp.concatenate([bh, bl, zeros], 0))
         leaf_c[leaf] = fold(prod[:ROWS] + prod[ROWS:])
-    copies[0].wait()
     for t in range(8):
         for g in range(8):
             low, high = slice(g * PTS, (g + 1) * PTS), slice(1024 + g * PTS, 1024 + (g + 1) * PTS)
             sums[t * ROWS : (t + 1) * ROWS, low] = (
-                one[t : t + 1, low] * leaf_c[2 * t] + one[t : t + 1, high] * leaf_c[2 * t + 1]
+                one_ref[rank, t : t + 1, low] * leaf_c[2 * t] + one_ref[rank, t : t + 1, high] * leaf_c[2 * t + 1]
             )
     one_c[...] = dot_two(sums[...], ones)
     strip_ref[:ROWS, FIRST] = pack(one_c[: 4 * ROWS], segment)
     strip_ref[:ROWS, LAST] = pack(one_c[4 * ROWS :], segment)
-    copies[1].wait()
-    two[...] = pltpu.roll(two[...], (rank % 2) * 4, 0)
     for t in range(4):
         for g in range(8):
             low, high = slice(g * PTS, (g + 1) * PTS), slice(1024 + g * PTS, 1024 + (g + 1) * PTS)
@@ -119,8 +128,7 @@
     top = pack(dot_two(sums[: 4 * ROWS], ones), segment)
     for copy in range(top_ref.shape[0]):
         top_ref[copy] = top
-    copies[2].wait()
-    strip_ref[ROWS : ROWS + 7, : OWN * PTS] = geo[...]
+    strip_ref[ROWS:, : OWN * PTS] = geo_ref[...]
 
 
 def couple_rows(coefs, first, row_of, sums):
@@ -143,7 +151,7 @@
     table[half:] = other_ref[...]
     for t in range(16):
         for j in range(COUPLE):
-            n = lists[t, j]
+            n = lists[j, t]
             live = (n >= 0) & (((n >> 2) & 3) == rank)
             group = jnp.where(live, n >> 4, 0)
             slot = jnp.where(live, n & 3, -1)
@@ -179,18 +187,12 @@
 
     def leaf(i):
         at = jnp.transpose(geo[OWN + i])
-        px, py, pz = (jnp.broadcast_to(at[:, k : k + 1], (PTS, PTS)) for k in range(3))
-        total = None
-        for j in range(NEAR):
-            n = near[rank * OWN + i, j]
+        spots = [jnp.broadcast_to(at[:, k : k + 1], (PTS, PTS)) for k in range(3)]
+        total = dot_last(block(*spots, geo[OWN + i]), weights[OWN + i])
+        for j in range(1, NEAR):
+            n = near[j, rank * OWN + i]
             s = jnp.where(n >= 0, jnp.clip(n - base, 0, 3 * OWN - 1), 3 * OWN)
-            src = geo[s]
-            dx, dy, dz = px - src[0:1], py - src[1:2], pz - src[2:3]
-            inv = lax.rsqrt(dx * dx + dy * dy + dz * dz + SOFTEN)
-            turn = dx * src[3:4] + dy * src[4:5] + dz * src[5:6]
-            high, low = split(inv + turn * (inv * inv * inv))
-            term = dot_last(jnp.concatenate([high, low], 1), weights[s])
-            total = term if j == 0 else total + term
+            total = total + dot_last(block(*spots, geo[s]), weights[s])
         flat = jnp.transpose(total)
         out_ref[:, pl.ds(pl.multiple_of(i * PTS, PTS), PTS)] = flat[:ROWS] + flat[ROWS:]
 
@@ -207,7 +209,7 @@
     first = place[2] * 8 - 4
     for t in range(8):
         for j in range(COUPLE):
-            n = lists[rank * 8 + t, j]
+            n = lists[j, rank * 8 + t]
             q = jnp.clip(n - first, 0, 15)
             coefs[t * COUPLE + j] = pick(table[q >> 2], segment, jnp.where(n >= 0, q & 3, -1))
     copy.wait()
@@ -218,7 +220,9 @@
         out_ref[:, at : at + PTS] = pack(total[part * 4 * ROWS : (part + 1) * 4 * ROWS], segment)
 
 
-def final_kernel(got, one_ref, two_ref, basis_ref, out_ref, spread_two, spread_one):
+def final_kernel(place, got, one_ref, two_ref, basis0, basis1, basis2, basis3, out_ref, spread_two, spread_one, basis_ref):
+    for s, ref in enumerate((basis0, basis1, basis2, basis3)):
+        basis_ref[pl.ds((place[0] ^ s) * OWN, OWN)] = ref[...]
     segment = lane_segment(8)
     lower = lax.broadcasted_iota(jnp.int32, (8, PTS), 0) < 4
 
@@ -283,25 +287,26 @@
     gathered = lax.axis_size("x") * lax.axis_size("z")
     place = jnp.stack([lax.axis_index("r"), lax.axis_index("c"), lax.axis_index(ALL)]).astype(jnp.int32)
 
-    basis_all = lax.all_gather(basis, "r", axis=0, tiled=True)
+    bases = [basis] + [lax.ppermute(basis, "r", [(i, i ^ s) for i in range(4)]) for s in range(1, 4)]
     val = lax.all_to_all(values, "r", split_axis=1, concat_axis=0, tiled=True)
+    geo, two = pl.pallas_call(
+        prepare_kernel,
+        in_specs=[SMEM, HBM, HBM],
+        out_specs=[VMEM] * 2,
+        out_shape=[shape(8, OWN * PTS), shape(8, 2048)],
+        scratch_shapes=[pltpu.SemaphoreType.DMA((2,))],
+        compiler_params=PARAMS,
+        cost_estimate=pl.CostEstimate(flops=1_000_000, bytes_accessed=300_000, transcendentals=0),
+    )(place, geometry, transfer_two.reshape(2, 8, 2048))
     strip, top = pl.pallas_call(
         up_kernel,
-        in_specs=[SMEM, VMEM, ANY, VMEM, ANY, ANY],
+        in_specs=[SMEM] + [VMEM] * 5,
         out_specs=[VMEM, VMEM],
         out_shape=[shape(*STRIP), shape(gathered, ROWS, PTS)],
-        scratch_shapes=[
-            scratch(OWN, ROWS, PTS),
-            scratch(8 * ROWS, PTS),
-            scratch(8 * ROWS, 1024),
-            scratch(7, OWN * PTS),
-            scratch(8, 2048),
-            scratch(8, 2048),
-            pltpu.SemaphoreType.DMA((3,)),
-        ],
+        scratch_shapes=[scratch(OWN, ROWS, PTS), scratch(8 * ROWS, PTS), scratch(8 * ROWS, 1024)],
         compiler_params=PARAMS,
         cost_estimate=pl.CostEstimate(flops=40_000_000, bytes_accessed=600_000, transcendentals=0),
-    )(place, val, geometry, basis, transfer_one.reshape(4, 8, 2048), transfer_two.reshape(2, 8, 2048))
+    )(place, val, geo, basis, transfer_one.reshape(4, 8, 2048), two)
 
     left = lax.ppermute(strip, ALL, [(i, i + 1) for i in range(size - 1)])
     right = lax.ppermute(strip, ALL, [(i + 1, i) for i in range(size - 1)])
@@ -310,7 +315,7 @@
 
     near_part = pl.pallas_call(
         near_kernel,
-        in_specs=[SMEM, SMEM, SMEM, VMEM, VMEM, VMEM, ANY],
+        in_specs=[SMEM] * 3 + [VMEM] * 3 + [HBM],
         out_specs=VMEM,
         out_shape=shape(ROWS, OWN * PTS + 2 * PTS),
         scratch_shapes=[
@@ -323,8 +328,8 @@
             pltpu.SemaphoreType.DMA(()),
         ],
         compiler_params=PARAMS,
-        cost_estimate=pl.CostEstimate(flops=3_000_000_000, bytes_accessed=700_000, transcendentals=1_600_000),
-    )(place, near, lists_one, left, strip, right, couple_one.reshape(4, 8, 8192))
+        cost_estimate=pl.CostEstimate(flops=30_000_000_000, bytes_accessed=700_000, transcendentals=1_600_000),
+    )(place, near.T, lists_one.T, left, strip, right, couple_one.reshape(4, 8, 8192))
 
     message = pl.pallas_call(
         couple_kernel,
@@ -338,18 +343,18 @@
         ],
         compiler_params=PARAMS,
         cost_estimate=pl.CostEstimate(flops=100_000_000, bytes_accessed=1_000_000, transcendentals=0),
-    )(place, lists_two, mine, other, couple_two, near_part)
+    )(place, lists_two.T, mine, other, couple_two, near_part)
     got = lax.all_to_all(message.reshape(4, 4, MESSAGE), "r", split_axis=0, concat_axis=0, tiled=True)
 
     return pl.pallas_call(
         final_kernel,
-        in_specs=[VMEM] * 4,
+        in_specs=[SMEM] + [VMEM] * 7,
         out_specs=VMEM,
         out_shape=shape(4, 4 * OWN * PTS),
-        scratch_shapes=[scratch(64, 1024), scratch(128, 1024)],
+        scratch_shapes=[scratch(64, 1024), scratch(128, 1024), scratch(4 * OWN, RANK, PTS)],
         compiler_params=PARAMS,
         cost_estimate=pl.CostEstimate(flops=40_000_000, bytes_accessed=2_000_000, transcendentals=0),
-    )(got, transfer_one, transfer_two, basis_all)
+    )(place, got, transfer_one, transfer_two, *bases)
 
 
 def solution(mesh):

time: 77.6 us -> 69.5 us (0.90)
  the two profiles are of different devices: /device:TPU:2 before, /device:TPU:33 now
where the time goes in v3:
time: 69.5 us; the launch traced here: 69 us
  starting transfers between devices  32.2 us (46%)
  waiting for transfers between devices  19 us (27%)
  Pallas kernels  16.8 us (24%)
  local copies, waits for them, and re-layouts  0.8 us (1%)
    all_to_all x1, starting transfers between devices, on_device(): lax.all_to_all(top, ('x', 'z'), split_axis=0, concat_axis=0, tiled=True)  10.8 us
    ppermute x1, waiting for transfers between devices, on_device(): left = lax.ppermute(strip, ALL, [(i, i + 1) for i in range(size - 1)])  9.85 us
    pallas_call x1, Pallas kernels, on_device(): pl.pallas_call(near_kernel, in_specs=[SMEM] * 3 + [VMEM] * 3 + [HBM], out...  9.46 us
    ppermute x1, starting transfers between devices, on_device(): right = lax.ppermute(strip, ALL, [(i + 1, i) for i in range(size - 1)])  5.35 us
    all_to_all x1, waiting for transfers between devices, on_device(): lax.all_to_all(message.reshape(4, 4, MESSAGE), 'r', split_axis=0, concat_...  5.02 us
    all_to_all x1, starting transfers between devices, on_device(): val = lax.all_to_all(values, 'r', split_axis=1, concat_axis=0, tiled=True)  4.33 us
    all_to_all x1, waiting for transfers between devices, on_device(): val = lax.all_to_all(values, 'r', split_axis=1, concat_axis=0, tiled=True)  4.07 us
    all_to_all x1, starting transfers between devices, on_device(): lax.all_to_all(message.reshape(4, 4, MESSAGE), 'r', split_axis=0, concat_...  3.35 us
  transfers between devices with their start and end apart: 9, of which 3 were waited for; matrix products, arithmetic and copies ran while one was open for 1% of the time, Pallas kernels for 18%

profile of v3, /device:TPU:33, one launch (start us, length us, event | category | flops | bytes accessed | tf_op | source)
XLA Modules:
  0.0 69.0 jit_solution(785254372077699315)
XLA Ops:
  0.0 0.0 copy-start.3
  0.0 0.0 copy-start.4
  0.0 0.0 copy-start.1
  0.0 4.3 %all-to-all-start = ((f32[4,4,2048]{2,0,1:T(4,128)}), f32[4,4,2048]{2,0,1:T(4,128)S(1)}, u32[]{:S(2)}, u32[]{:S(2)}) async-start(f32[4,4,2048]{2,0,1:T(4,128)} %bitcast.18), calls=%async_computation | async-start | bytes 262144 | tf_op jit(solution)/shard_map/all_to_all | solution.py:291
  4.3 0.0 copy-start
  4.3 0.0 copy-start.6
  4.3 0.1 pad_add_fusion.place
  4.4 0.0 copy-done.3
  4.4 0.0 copy-done.4
  4.4 0.7 shard_map.100
  5.1 4.1 %all-to-all-done = f32[4,4,2048]{2,0,1:T(4,128)S(1)} async-done(((f32[4,4,2048]{2,0,1:T(4,128)}), f32[4,4,2048]{2,0,1:T(4,128)S(1)}, u32[]{:S(2)}, u32[]{:S(2)}) %all-to-all-start) | async-done | bytes 131104 | tf_op jit(solution)/shard_map/all_to_all | solution.py:291
  9.2 0.0 copy-done.1
  9.2 0.0 copy-done
  9.2 2.1 %shard_map.101 = (f32[24,2304]{1,0:T(8,128)S(1)}, f32[32,16,128]{2,1,0:T(8,128)}) custom-call(s32[3]{0:T(128)S(1)} %pad_add_fusion.place, f32[16,2048]{1,0:T(8,128)S(1)} %all_to_all.23.v_ref, f32[8,2048]{1,0:T(8,128)S(1)} %get-tuple-element.9.geo_ref, f32[16,32,128]{2,1,0:T(8,128)S(1)} %copy-done, f32[4,8,2048]{2,1,0:T(8,128)S(1)} %bitcast.11, ...), custom_call_target="tpu_custom_call" | custom-call | flops 40000000 | bytes 600000 | tf_op jit(solution)/shard_map/pallas_call | solution.py:301
  11.4 0.0 copy-start.8
  11.4 10.8 %all-to-all-start.1 = ((f32[32,16,128]{2,1,0:T(8,128)}), f32[32,16,128]{2,1,0:T(8,128)S(1)}, u32[]{:S(2)}, u32[]{:S(2)}) async-start(f32[32,16,128]{2,1,0:T(8,128)} %get-tuple-element.11), calls=%async_computation.1 | async-start | bytes 524288 | tf_op jit(solution)/shard_map/all_to_all | solution.py:313
  22.1 0.0 copy-start.7
  22.1 5.3 %collective-permute-start.2 = (f32[24,2304]{1,0:T(8,128)S(1)}, f32[24,2304]{1,0:T(8,128)S(1)}, u32[]{:S(2)}, u32[]{:S(2)}) collective-permute-start(f32[24,2304]{1,0:T(8,128)S(1)} %get-tuple-element.12.own), channel_id=1, source_target_pairs={{1,0},{2,1},{3,2},{4,3},{5,4},{6,5},{7,6},{8,7},{9,8},{10,9},{11,1... | collective-permute-start | bytes 663560 | tf_op jit(solution)/shard_map/ppermute | solution.py:312
  27.5 1.9 %collective-permute-start.1 = (f32[24,2304]{1,0:T(8,128)S(1)}, f32[24,2304]{1,0:T(8,128)}, u32[]{:S(2)}, u32[]{:S(2)}) collective-permute-start(f32[24,2304]{1,0:T(8,128)S(1)} %get-tuple-element.12.own), channel_id=1, source_target_pairs={{0,1},{1,2},{2,3},{3,4},{4,5},{5,6},{6,7},{7,8},{8,9},{9,10},{10,1... | collective-permute-start | bytes 663560 | tf_op jit(solution)/shard_map/ppermute | solution.py:311
  29.4 0.1 collective-permute-start.4
  29.5 3.2 %collective-permute-start.3 = (f32[16,32,128]{2,1,0:T(8,128)S(1)}, f32[16,32,128]{2,1,0:T(8,128)S(1)}, u32[]{:S(2)}, u32[]{:S(2)}) collective-permute-start(f32[16,32,128]{2,1,0:T(8,128)S(1)} %copy-done), channel_id=1, source_target_pairs={{0,1},{1,0},{2,3},{3,2},{4,5},{5,4},{6,7},{7,6},{8,9},{9,8},{10,11... | collective-permute-start | bytes 786440 | tf_op jit(solution)/shard_map/ppermute | solution.py:290
  32.8 0.0 collective-permute-start.5
  32.8 0.0 collective-permute-done.2.right
  32.8 0.0 all-to-all-done.1.mine_ref
  32.8 3.1 %collective-permute-start = (f32[32,16,128]{2,1,0:T(8,128)S(1)}, f32[32,16,128]{2,1,0:T(8,128)S(1)}, u32[]{:S(2)}, u32[]{:S(2)}) collective-permute-start(f32[32,16,128]{2,1,0:T(8,128)S(1)} %all-to-all-done.1.mine_ref), channel_id=1, source_target_pairs={{0,4},{4,0},{1,5},{5,1},{2,6},{6,2},{3,7},{7,3},{8,12},{12,8},{9,1... | collective-permute-start | bytes 786440 | tf_op jit(solution)/shard_map/ppermute | solution.py:314
  35.9 9.9 %collective-permute-done.1.left = f32[24,2304]{1,0:T(8,128)} collective-permute-done((f32[24,2304]{1,0:T(8,128)S(1)}, f32[24,2304]{1,0:T(8,128)}, u32[]{:S(2)}, u32[]{:S(2)}) %collective-permute-start.1) | collective-permute-done | bytes 221216 | tf_op jit(solution)/shard_map/ppermute | solution.py:311
  45.8 0.0 copy-done.6
  45.8 0.0 copy-done.8
  45.8 0.0 copy-done.7
  45.8 0.0 copy-start.2
  45.8 0.0 copy-start.5
  45.8 9.5 %shard_map.102.near_ref = f32[16,2304]{1,0:T(8,128)S(1)} custom-call(s32[3]{0:T(128)S(1)} %pad_add_fusion.place, s32[6,64]{1,0:T(8,128)S(1)} %bitcast.15, s32[8,32]{1,0:T(8,128)S(1)} %bitcast.16, f32[24,2304]{1,0:T(8,128)} %collective-permute-done.1.left, f32[24,2304]{1,0:T(8,128)S(1)} %get-tuple-element.12.own, ...), custom_call_target="tpu_custom_call" | custom-call | flops 30000001024 | bytes 700000 | tf_op jit(solution)/shard_map/pallas_call | solution.py:316
  55.3 0.0 collective-permute-done.other_ref
  55.3 0.0 copy-done.2
  55.3 0.0 copy-done.5
  55.3 2.1 %shard_map.103 = f32[16,2816]{1,0:T(8,128)S(1)} custom-call(s32[3]{0:T(128)S(1)} %pad_add_fusion.place, s32[8,16]{1,0:T(8,128)S(1)} %bitcast.13, f32[32,16,128]{2,1,0:T(8,128)S(1)} %all-to-all-done.1.mine_ref, f32[32,16,128]{2,1,0:T(8,128)S(1)} %collective-permute-done.other_ref, f32[16,8192]{1,0:T(8,128)S(1)} %copy-done.2, f32[16,2304]{1,0:T(8,128)S(1)} %shard_map.102.near_ref), custom_call_target="tpu_custom_call" | custom-call | flops 100000000 | bytes 1000000 | tf_op jit(solution)/shard_map/pallas_call | solution.py:334
  57.4 0.7 %reshape.18 = f32[4,4,2816]{2,1,0:T(4,128)} reshape(f32[16,2816]{1,0:T(8,128)S(1)} %shard_map.103) | data formatting | bytes 360448 | tf_op jit(solution)/shard_map/reshape | solution.py:347
  58.1 3.4 %all-to-all-start.2 = ((f32[4,4,2816]{2,1,0:T(4,128)}), f32[4,4,2816]{2,1,0:T(4,128)S(1)}, u32[]{:S(2)}, u32[]{:S(2)}) async-start(f32[4,4,2816]{2,1,0:T(4,128)} %reshape.18), calls=%async_computation.2 | async-start | bytes 360448 | tf_op jit(solution)/shard_map/all_to_all | solution.py:347
  61.4 0.0 collective-permute-done.4.basis2
  61.5 0.0 collective-permute-done.3.basis1
  61.5 0.0 collective-permute-done.5.basis3
  61.5 5.0 %all-to-all-done.2.got = f32[4,4,2816]{2,1,0:T(4,128)S(1)} async-done(((f32[4,4,2816]{2,1,0:T(4,128)}), f32[4,4,2816]{2,1,0:T(4,128)S(1)}, u32[]{:S(2)}, u32[]{:S(2)}) %all-to-all-start.2) | async-done | bytes 180256 | tf_op jit(solution)/shard_map/all_to_all | solution.py:347
  66.5 2.5 %shard_map.104 = f32[4,8192]{1,0:T(4,128)} custom-call(s32[3]{0:T(128)S(1)} %pad_add_fusion.place, f32[4,4,2816]{2,1,0:T(4,128)S(1)} %all-to-all-done.2.got, f32[32,2048]{1,0:T(8,128)S(1)} %copy-done.1, f32[16,2048]{1,0:T(8,128)S(1)} %copy-done.3, f32[16,32,128]{2,1,0:T(8,128)S(1)} %copy-done, f32[16,32,128]{2,1,0:T(8,128)S(1)} %collective-permute-done.3.basis1, ...), custom_call_target="tpu_custom_call" | custom-call | flops 40000000 | bytes 2000000 | tf_op jit(solution)/shard_map/pallas_call | solution.py:349
  (1 shorter events, 0.0 us)
Async XLA Ops:
  0.0 4.4 %copy-start.3 = (f32[16,2048]{1,0:T(8,128)S(1)}, f32[16,2048]{1,0:T(8,128)}, u32[]{:S(2)}) copy-start(f32[16,2048]{1,0:T(8,128)} %two_ref.1) | copy-start | bytes 393220
  0.0 4.4 %copy-start.4 = (f32[7,2048]{1,0:T(8,128)S(1)}, f32[7,2048]{1,0:T(8,128)}, u32[]{:S(2)}) copy-start(f32[7,2048]{1,0:T(8,128)} %geo_hbm.1) | copy-start | bytes 172036
  0.0 9.2 %copy-start.1 = (f32[32,2048]{1,0:T(8,128)S(1)}, f32[32,2048]{1,0:T(8,128)}, u32[]{:S(2)}) copy-start(f32[32,2048]{1,0:T(8,128)} %one_ref.1) | copy-start | bytes 786436
  0.0 9.2 %all-to-all-start = ((f32[4,4,2048]{2,0,1:T(4,128)}), f32[4,4,2048]{2,0,1:T(4,128)S(1)}, u32[]{:S(2)}, u32[]{:S(2)}) async-start(f32[4,4,2048]{2,0,1:T(4,128)} %bitcast.18), calls=%async_computation | async-start | bytes 262144 | tf_op jit(solution)/shard_map/all_to_all | solution.py:291
  4.3 4.9 %copy-start = (f32[16,32,128]{2,1,0:T(8,128)S(1)}, f32[16,32,128]{2,1,0:T(8,128)}, u32[]{:S(2)}) copy-start(f32[16,32,128]{2,1,0:T(8,128)} %basis0.1) | copy-start | bytes 786436
  4.3 41.4 %copy-start.6 = (f32[32,8192]{1,0:T(8,128)S(1)}, f32[32,8192]{1,0:T(8,128)}, u32[]{:S(2)}) copy-start(f32[32,8192]{1,0:T(8,128)} %param.16) | copy-start | bytes 3145732
  11.4 34.4 %copy-start.8 = (s32[32,8]{0,1:T(8,128)S(1)}, s32[32,8]{0,1:T(8,128)}, u32[]{:S(2)}) copy-start(s32[32,8]{0,1:T(8,128)} %param.18) | copy-start | bytes 3076
  11.4 21.4 %all-to-all-start.1 = ((f32[32,16,128]{2,1,0:T(8,128)}), f32[32,16,128]{2,1,0:T(8,128)S(1)}, u32[]{:S(2)}, u32[]{:S(2)}) async-start(f32[32,16,128]{2,1,0:T(8,128)} %get-tuple-element.11), calls=%async_computation.1 | async-start | bytes 524288 | tf_op jit(solution)/shard_map/all_to_all | solution.py:313
  22.1 23.6 %copy-start.7 = (s32[64,6]{0,1:T(8,128)S(1)}, s32[64,6]{0,1:T(8,128)}, u32[]{:S(2)}) copy-start(s32[64,6]{0,1:T(8,128)} %param.13) | copy-start | bytes 4612
  22.1 10.6 %collective-permute-start.2 = (f32[24,2304]{1,0:T(8,128)S(1)}, f32[24,2304]{1,0:T(8,128)S(1)}, u32[]{:S(2)}, u32[]{:S(2)}) collective-permute-start(f32[24,2304]{1,0:T(8,128)S(1)} %get-tuple-element.12.own), channel_id=1, source_target_pairs={{1,0},{2,1},{3,2},{4,3},{5,4},{6,5},{7,6},{8,7},{9,8},{10,9},{11,1... | collective-permute-start | bytes 663560 | tf_op jit(solution)/shard_map/ppermute | solution.py:312
  27.5 18.3 %collective-permute-start.1 = (f32[24,2304]{1,0:T(8,128)S(1)}, f32[24,2304]{1,0:T(8,128)}, u32[]{:S(2)}, u32[]{:S(2)}) collective-permute-start(f32[24,2304]{1,0:T(8,128)S(1)} %get-tuple-element.12.own), channel_id=1, source_target_pairs={{0,1},{1,2},{2,3},{3,4},{4,5},{5,6},{6,7},{7,8},{8,9},{9,10},{10,1... | collective-permute-start | bytes 663560 | tf_op jit(solution)/shard_map/ppermute | solution.py:311
  29.4 32.0 %collective-permute-start.4 = (f32[16,32,128]{2,1,0:T(8,128)S(1)}, f32[16,32,128]{2,1,0:T(8,128)S(1)}, u32[]{:S(2)}, u32[]{:S(2)}) collective-permute-start(f32[16,32,128]{2,1,0:T(8,128)S(1)} %copy-done), channel_id=1, source_target_pairs={{0,2},{1,3},{2,0},{3,1},{4,6},{5,7},{6,4},{7,5},{8,10},{9,11},{10,... | collective-permute-start | bytes 786440 | tf_op jit(solution)/shard_map/ppermute | solution.py:290
  29.5 31.9 %collective-permute-start.3 = (f32[16,32,128]{2,1,0:T(8,128)S(1)}, f32[16,32,128]{2,1,0:T(8,128)S(1)}, u32[]{:S(2)}, u32[]{:S(2)}) collective-permute-start(f32[16,32,128]{2,1,0:T(8,128)S(1)} %copy-done), channel_id=1, source_target_pairs={{0,1},{1,0},{2,3},{3,2},{4,5},{5,4},{6,7},{7,6},{8,9},{9,8},{10,11... | collective-permute-start | bytes 786440 | tf_op jit(solution)/shard_map/ppermute | solution.py:290
  32.8 28.7 %collective-permute-start.5 = (f32[16,32,128]{2,1,0:T(8,128)S(1)}, f32[16,32,128]{2,1,0:T(8,128)S(1)}, u32[]{:S(2)}, u32[]{:S(2)}) collective-permute-start(f32[16,32,128]{2,1,0:T(8,128)S(1)} %copy-done), channel_id=1, source_target_pairs={{0,3},{1,2},{2,1},{3,0},{4,7},{5,6},{6,5},{7,4},{8,11},{9,10},{10,... | collective-permute-start | bytes 786440 | tf_op jit(solution)/shard_map/ppermute | solution.py:290
  32.8 22.5 %collective-permute-start = (f32[32,16,128]{2,1,0:T(8,128)S(1)}, f32[32,16,128]{2,1,0:T(8,128)S(1)}, u32[]{:S(2)}, u32[]{:S(2)}) collective-permute-start(f32[32,16,128]{2,1,0:T(8,128)S(1)} %all-to-all-done.1.mine_ref), channel_id=1, source_target_pairs={{0,4},{4,0},{1,5},{5,1},{2,6},{6,2},{3,7},{7,3},{8,12},{12,8},{9,1... | collective-permute-start | bytes 786440 | tf_op jit(solution)/shard_map/ppermute | solution.py:314
  45.8 9.5 %copy-start.2 = (f32[16,8192]{1,0:T(8,128)S(1)}, f32[16,8192]{1,0:T(8,128)}, u32[]{:S(2)}) copy-start(f32[16,8192]{1,0:T(8,128)} %mats_ref.1) | copy-start | bytes 1572868
  45.8 9.5 %copy-start.5 = (s32[16,8]{0,1:T(8,128)S(1)}, s32[16,8]{0,1:T(8,128)}, u32[]{:S(2)}) copy-start(s32[16,8]{0,1:T(8,128)} %param.19) | copy-start | bytes 1540
  58.1 8.4 %all-to-all-start.2 = ((f32[4,4,2816]{2,1,0:T(4,128)}), f32[4,4,2816]{2,1,0:T(4,128)S(1)}, u32[]{:S(2)}, u32[]{:S(2)}) async-start(f32[4,4,2816]{2,1,0:T(4,128)} %reshape.18), calls=%async_computation.2 | async-start | bytes 360448 | tf_op jit(solution)/shard_map/all_to_all | solution.py:347
